TPU v7x, 512 devices: a whole 4x8x8 slice. The times are simulated.
512 devices in a mesh: tile: 64 (over y_hi, z, core), kern: 8 (over x, y_lo).
Axes of the slice: x: 4, y: 8 (y_hi: 4, y_lo: 2; y = y_hi * 2 + y_lo), z: 8, core: 2. Of those that a mesh axis runs over, the one named last changes fastest.
Arguments:
- levels: int32 [4096, 256], P('tile'), may hold values from 0 to 3
- jitter: float32 [4096, 256], P('tile'), may hold values from -6 to 6
- target: int32 [4096, 256], P('tile'), may hold values 0 or 1
- kernels: bfloat16 [24, 2, 35, 35], P('kern'), may hold values from -0.03125 to 0.03125
- kernel_weight: float32 [24], P('kern'), may hold values from 0.3 to 1
Outputs:
- mask_grad: float32 [4096, 256], P('tile', 'kern')
All inputs are finite; a program needn't handle non-finite values. No bound on the sum of `target` on one device may be relied on, other than what follows from the above.
Results may differ from a plain program's by a relative error of at most 0.003.
Values may be sent and summed in bfloat16 or wider, within the bound.
No kernel may reach another device: no remote copies, remote signals or barrier semaphores. Data moves between devices by JAX's collectives and lax.ppermute only.
A program may use at most 128 MiB of HBM per device.

v0:
```python
import jax
import jax.numpy as jnp
from jax import lax
from jax.sharding import PartitionSpec as P

steepness = 10.0
threshold = 0.4
block_rows = 32


def extended_2(cells, sides, width):
    for axis, dim in sides:
        count = lax.axis_size(axis)
        ends = count - 1
        head = lax.slice_in_dim(cells, 0, width, axis=dim)
        tail = lax.slice_in_dim(cells, cells.shape[dim] - width, cells.shape[dim], axis=dim)
        cells = jnp.concatenate(
            [
                lax.ppermute(tail, axis, [(i, (i + 1) % count) for i in range(ends)]),
                cells,
                lax.ppermute(head, axis, [((i + 1) % count, i) for i in range(ends)]),
            ],
            axis=dim,
        )
    return cells


def band_matrix(kernels):
    tap_count = kernels.shape[-1]
    span_cols = 128 + tap_count - 1
    shape3 = (span_cols, 128, tap_count)
    offsets = lax.broadcasted_iota(jnp.int32, shape3, 0) - lax.broadcasted_iota(
        jnp.int32, shape3, 1
    )
    select = (offsets == lax.broadcasted_iota(jnp.int32, shape3, 2)).astype(jnp.float32)
    matrix = jnp.einsum("kpij,qcj->iqkpc", kernels.astype(jnp.float32), select)
    return matrix.reshape(tap_count * span_cols, -1).astype(jnp.bfloat16)


def band_forward(padded, matrix, out_rows, tap_count):
    half_taps = tap_count // 2
    full_width = padded.shape[1]
    block_count = full_width // 128
    span_cols = 128 + tap_count - 1
    row_blocks = -(-out_rows // block_rows)
    extra = row_blocks * block_rows - out_rows
    widened = jnp.pad(padded, ((0, extra), (half_taps, half_taps)))

    def forward_block(block_index):
        rows_in = lax.dynamic_slice_in_dim(
            widened, block_index * block_rows, block_rows + tap_count - 1, 0
        )
        shifted = jnp.stack([rows_in[i : i + block_rows] for i in range(tap_count)], 1)
        col_blocks = jnp.stack(
            [shifted[:, :, 128 * b : 128 * b + span_cols] for b in range(block_count)], 1
        )
        return jnp.dot(
            col_blocks.reshape(block_rows * block_count, tap_count * span_cols),
            matrix,
            preferred_element_type=jnp.float32,
        )

    result = lax.map(forward_block, jnp.arange(row_blocks, dtype=jnp.int32))
    result = result.reshape(row_blocks * block_rows, block_count, -1, 128)
    return result.transpose(2, 0, 1, 3).reshape(-1, out_rows, block_count * 128)


def band_adjoint(extended, matrix, row_count, tap_count):
    channels, in_rows, full_width = extended.shape
    half_taps = tap_count // 2
    block_count = full_width // 128
    span_cols = 128 + tap_count - 1
    row_blocks = -(-in_rows // block_rows)
    extra = row_blocks * block_rows - in_rows
    arranged = jnp.pad(extended, ((0, 0), (0, extra), (0, 0)))
    arranged = arranged.reshape(channels, row_blocks, block_rows, block_count, 128)
    arranged = arranged.transpose(1, 2, 3, 0, 4).reshape(
        row_blocks, block_rows * block_count, channels * 128
    )
    accumulated = jnp.zeros(
        (row_blocks * block_rows + tap_count - 1, full_width + tap_count - 1), jnp.float32
    )

    def adjoint_block(carried, inputs):
        piece, block_index = inputs
        spread = lax.dot_general(
            piece, matrix, (((1,), (1,)), ((), ())), preferred_element_type=jnp.float32
        )
        spread = spread.reshape(block_rows, block_count, tap_count, span_cols)
        row_sum = jnp.pad(spread[:, :, 0, :], ((0, tap_count - 1), (0, 0), (0, 0)))
        for i in range(1, tap_count):
            row_sum = row_sum + jnp.pad(
                spread[:, :, i, :], ((i, tap_count - 1 - i), (0, 0), (0, 0))
            )
        placed = jnp.pad(row_sum[:, 0, :], ((0, 0), (0, full_width - 128)))
        placed = placed + jnp.pad(row_sum[:, 1, :], ((0, 0), (128, full_width - 128 - 128)))
        start = (block_index * block_rows, jnp.zeros((), jnp.int32))
        current = lax.dynamic_slice(carried, start, placed.shape)
        return (lax.dynamic_update_slice(carried, current + placed, start), None)

    accumulated, _ = lax.scan(
        adjoint_block, accumulated, (arranged, jnp.arange(row_blocks, dtype=jnp.int32))
    )
    return accumulated[
        2 * half_taps : 2 * half_taps + row_count, half_taps : half_taps + full_width
    ]


def resist_drive(intensity, target_rows):
    resist = jax.nn.sigmoid(steepness * (intensity - threshold))
    return 2.0 * (resist - target_rows) * steepness * resist * (1.0 - resist)


def on_device(levels, jitter, target, kernels, kernel_weight):
    tap_count = kernels.shape[-1]
    half_taps = tap_count // 2
    row_count, full_width = levels.shape
    mask_field = jax.nn.sigmoid(levels.astype(jnp.float32) - 1.5 + jitter).astype(jnp.bfloat16)
    matrix = band_matrix(kernels)
    weights = jnp.repeat(kernel_weight, 2)
    padded = extended_2(mask_field, (("tile", 0),), half_taps)
    target_rows = target.astype(jnp.float32)
    fields = band_forward(padded, matrix, row_count, tap_count)
    partial_sum = jnp.sum(weights[:, None, None] * fields * fields, axis=0)
    intensity = lax.psum(partial_sum, "kern")
    drive_field = resist_drive(intensity, target_rows)
    adjoint = ((2.0 * weights)[:, None, None] * drive_field * fields).astype(jnp.bfloat16)
    adjoint_ext = extended_2(adjoint, (("tile", 1),), half_taps)
    local_grad = band_adjoint(adjoint_ext, matrix, row_count, tap_count)
    return lax.psum_scatter(local_grad, "kern", scatter_dimension=1, tiled=True)


def solution(mesh):
    return jax.shard_map(
        on_device,
        mesh=mesh,
        in_specs=(
            P("tile", None),
            P("tile", None),
            P("tile", None),
            P("kern", None, None, None),
            P("kern"),
        ),
        out_specs=P("tile", "kern"),
        check_vma=False,
    )
```

profile of v0, /device:TPU:56, one launch (start us, length us, event | category | flops | bytes accessed | tf_op | source)
XLA Modules:
  0.0 300.4 jit_solution(9755077726953114391)
XLA Ops:
  6.5 0.9 divide_convert_fusion
  7.5 1.9 collective-permute-start
  9.4 12.0 %collective-permute-start.1 = (bf16[17,256]{1,0:T(8,128)(2,1)S(1)}, bf16[17,256]{1,0:T(8,128)(2,1)S(1)}, u32[]{:S(2)}, u32[]{:S(2)}) collective-permute-start(bf16[17,256]{1,0:T(8,128)(2,1)S(1)} %get-tuple-element.161), channel_id=1, source_target_pairs={{8,0},{16,8},{24,16},{32,24},{40,32},{48,40},{56,48},{64,56},{72,6... | collective-permute-start | bytes 26120 | tf_op jit(solution)/shard_map/ppermute | solution.py:21
  21.4 6.1 %convert_bitcast_fusion = bf16[35,162,3,2,128]{4,0,3,2,1:T(8,128)(2,1)} fusion(bf16[3,2,35,35]{3,1,2,0:T(2,128)(2,1)} %param.12), kind=kOutput, calls=%fused_computation.117 | convolution fusion | flops 310625280 | bytes 8723820 | tf_op jit(solution)/shard_map/kpij,qcj->iqkpc/dot_general | solution.py:36
  27.4 14.0 %copy.79 = bf16[35,162,3,2,128]{4,3,2,1,0:T(2,128)(2,1)} copy(bf16[35,162,3,2,128]{4,0,3,2,1:T(8,128)(2,1)} %convert_bitcast_fusion) | data formatting | bytes 17418240 | tf_op jit(solution)/shard_map/convert_element_type | solution.py:37
  41.4 19.6 %convert_element_type.107 = bf16[5670,768]{1,0:T(8,128)(2,1)} reshape(bf16[35,162,3,2,128]{4,3,2,1,0:T(2,128)(2,1)} %copy.79) | data formatting | bytes 17418240 | tf_op jit(solution)/shard_map/convert_element_type | solution.py:37
  61.2 18.6 %while.22 = (s32[]{:T(128)}, f32[2,64,768]{2,1,0:T(8,128)S(1)}, s32[2]{0:T(128)S(1)}, bf16[98,290]{1,0:T(8,128)(2,1)S(1)}, bf16[5670,768]{1,0:T(8,128)(2,1)}, /*...) while((s32[]{:T(128)}, f32[2,64,768]{2,1,0:T(8,128)S(1)}, ...), condition=%wide.region_1.2_spmd, body=%wide.region_0.1_spmd.sunk | while | flops 557746624 | bytes 17164368 | solution.py:63
  61.2 0.7 dynamic_slice.33
  64.0 0.7 copy.132
  64.7 1.0 reshape.54
  65.7 4.9 %fusion.32 = f32[2,64,768]{2,1,0:T(8,128)S(1)} fusion(f32[2,64,768]{2,1,0:T(8,128)S(1)} %get-tuple-element.346, s32[]{:T(128)} %get-tuple-element.345, bf16[64,5670]{1,0:T(8,128)(2,1)S(1)} %reshape.54, bf16[5670,768]{1,0:T(8,128)(2,1)} %get-tuple-element.392), kind=kOutput, calls=%fused_computation.1.clone.1 | convolution fusion | flops 557383680 | bytes 9643012 | tf_op jit(solution)/shard_map/while/body/eval_jaxpr/dot_general | solution.py:57
  70.6 0.7 dynamic_slice.33
  73.4 0.7 copy.132
  74.0 1.0 reshape.54
  75.0 4.9 %fusion.32 = f32[2,64,768]{2,1,0:T(8,128)S(1)} fusion(f32[2,64,768]{2,1,0:T(8,128)S(1)} %get-tuple-element.346, s32[]{:T(128)} %get-tuple-element.345, bf16[64,5670]{1,0:T(8,128)(2,1)S(1)} %reshape.54, bf16[5670,768]{1,0:T(8,128)(2,1)} %get-tuple-element.392), kind=kOutput, calls=%fused_computation.1.clone.1 | convolution fusion | flops 557383680 | bytes 9643012 | tf_op jit(solution)/shard_map/while/body/eval_jaxpr/dot_general | solution.py:57
  79.9 0.3 fusion.8
  80.2 0.6 copy.129
  81.1 0.3 reshape.44
  81.5 77.6 %all-reduce.41.cloned.1.call-done = f32[64,256]{1,0:T(8,128)} async-done(((f32[64,256]{1,0:T(8,128)}), f32[64,256]{1,0:T(8,128)}) %all-reduce.41.cloned.1.call-update) | async-done | bytes 65552 | tf_op jit(solution)/shard_map/psum | solution.py:125
  159.0 0.9 subtract_multiply_fusion
  160.0 1.9 collective-permute-start.2
  162.0 6.8 %collective-permute-start.3 = (bf16[6,17,256]{2,1,0:T(8,128)(2,1)S(1)}, bf16[6,17,256]{2,1,0:T(8,128)(2,1)S(1)}, u32[]{:S(2)}, u32[]{:S(2)}) collective-permute-start(bf16[6,17,256]{2,1,0:T(8,128)(2,1)S(1)} %get-tuple-element.159), channel_id=1, source_target_pairs={{8,0},{16,8},{24,16},{32,24},{40,32},{48,40},{56,48},{64,56},{72,6... | collective-permute-start | bytes 156680 | tf_op jit(solution)/shard_map/ppermute | solution.py:21
  168.8 1.8 collective-permute-done.3
  170.8 0.5 copy.81
  171.3 0.5 reshape.46
  171.8 81.2 %while.23 = (s32[]{:T(128)}, f32[162,290]{1,0:T(8,128)S(1)}, s32[4]{0:T(128)S(1)}, bf16[4,64,768]{2,1,0:T(8,128)(2,1)S(1)}, bf16[5670,768]{1,0:T(8,128)(2,1)}, /...) while((s32[]{:T(128)}, f32[162,290]{1,0:T(8,128)S(1)}, s32[4]{0:T(128)S(1)}, ...), condition=%wide.region_5.6_spmd, body=%wide.region_4.5_spmd.sunk | while | flops 558148992 | bytes 33073504 | solution.py:101
  171.9 11.0 %reshape.55 = bf16[35,162,768,1]{2,1,0,3:T(8,128)(2,1)} reshape(bf16[5670,768]{1,0:T(8,128)(2,1)} %get-tuple-element.453) | data formatting | bytes 17418240 | tf_op jit(solution)/shard_map/while/body/eval_jaxpr/dot_general | solution.py:86
  182.9 6.6 %fusion.35 = f32[32,2,35,162]{3,0,2,1:T(8,128)S(1)} fusion(bf16[35,162,768,1]{2,1,0,3:T(8,128)(2,1)} %reshape.55, bf16[32,2,768,1]{2,1,0,3:T(2,128)(2,1)S(1)} %bitcast.405), kind=kOutput, calls=%fused_computation.77.clone.1 | convolution fusion | flops 557383680 | bytes 10258944 | tf_op jit(solution)/shard_map/while/body/eval_jaxpr/dot_general | solution.py:86
  189.6 0.4 pad_add_fusion.2
  190.0 0.7 dynamic_slice.36
  191.3 0.9 dynamic_update_slice.14
  192.3 11.0 %reshape.55 = bf16[35,162,768,1]{2,1,0,3:T(8,128)(2,1)} reshape(bf16[5670,768]{1,0:T(8,128)(2,1)} %get-tuple-element.453) | data formatting | bytes 17418240 | tf_op jit(solution)/shard_map/while/body/eval_jaxpr/dot_general | solution.py:86
  203.3 6.6 %fusion.35 = f32[32,2,35,162]{3,0,2,1:T(8,128)S(1)} fusion(bf16[35,162,768,1]{2,1,0,3:T(8,128)(2,1)} %reshape.55, bf16[32,2,768,1]{2,1,0,3:T(2,128)(2,1)S(1)} %bitcast.405), kind=kOutput, calls=%fused_computation.77.clone.1 | convolution fusion | flops 557383680 | bytes 10258944 | tf_op jit(solution)/shard_map/while/body/eval_jaxpr/dot_general | solution.py:86
  210.1 0.4 pad_add_fusion.2
  210.5 0.7 dynamic_slice.36
  211.8 0.8 dynamic_update_slice.14
  212.7 11.0 %reshape.55 = bf16[35,162,768,1]{2,1,0,3:T(8,128)(2,1)} reshape(bf16[5670,768]{1,0:T(8,128)(2,1)} %get-tuple-element.453) | data formatting | bytes 17418240 | tf_op jit(solution)/shard_map/while/body/eval_jaxpr/dot_general | solution.py:86
  223.7 6.6 %fusion.35 = f32[32,2,35,162]{3,0,2,1:T(8,128)S(1)} fusion(bf16[35,162,768,1]{2,1,0,3:T(8,128)(2,1)} %reshape.55, bf16[32,2,768,1]{2,1,0,3:T(2,128)(2,1)S(1)} %bitcast.405), kind=kOutput, calls=%fused_computation.77.clone.1 | convolution fusion | flops 557383680 | bytes 10258944 | tf_op jit(solution)/shard_map/while/body/eval_jaxpr/dot_general | solution.py:86
  230.5 0.4 pad_add_fusion.2
  230.9 0.7 dynamic_slice.36
  232.2 0.7 dynamic_update_slice.14
  233.0 11.0 %reshape.55 = bf16[35,162,768,1]{2,1,0,3:T(8,128)(2,1)} reshape(bf16[5670,768]{1,0:T(8,128)(2,1)} %get-tuple-element.453) | data formatting | bytes 17418240 | tf_op jit(solution)/shard_map/while/body/eval_jaxpr/dot_general | solution.py:86
  244.0 6.6 %fusion.35 = f32[32,2,35,162]{3,0,2,1:T(8,128)S(1)} fusion(bf16[35,162,768,1]{2,1,0,3:T(8,128)(2,1)} %reshape.55, bf16[32,2,768,1]{2,1,0,3:T(2,128)(2,1)S(1)} %bitcast.405), kind=kOutput, calls=%fused_computation.77.clone.1 | convolution fusion | flops 557383680 | bytes 10258944 | tf_op jit(solution)/shard_map/while/body/eval_jaxpr/dot_general | solution.py:86
  250.8 0.4 pad_add_fusion.2
  251.2 0.7 dynamic_slice.36
  252.5 0.5 dynamic_update_slice.14
  253.2 0.7 slice.396
  253.9 39.6 %reduce-scatter.2.cloned.1.call-done = f32[64,32]{0,1:T(8,128)} async-done(((f32[64,256]{0,1:T(8,128)}), f32[64,32]{0,1:T(8,128)}) %reduce-scatter.2.cloned.1.call-update) | async-done | bytes 8208 | tf_op jit(solution)/shard_map/reduce_scatter | solution.py:130
  (125 shorter events, 4.7 us)
Async XLA Ops:
  6.5 152.5 %all-reduce.41.cloned.1.call-start = ((), (), s32[]{:S(2)}) async-start(), calls=%async_computation.1 | async-start | bytes 131072 | tf_op jit(solution)/shard_map/psum | solution.py:125
  7.5 53.7 %collective-permute-start = (bf16[17,256]{1,0:T(8,128)(2,1)S(1)}, bf16[17,256]{1,0:T(8,128)(2,1)S(1)}, u32[]{:S(2)}, u32[]{:S(2)}) collective-permute-start(bf16[17,256]{1,0:T(8,128)(2,1)S(1)} %get-tuple-element.160), channel_id=1, source_target_pairs={{0,8},{8,16},{16,24},{24,32},{32,40},{40,48},{48,56},{56,64},{64,7... | collective-permute-start | bytes 26120 | tf_op jit(solution)/shard_map/ppermute | solution.py:19
  9.4 51.7 %collective-permute-start.1 = (bf16[17,256]{1,0:T(8,128)(2,1)S(1)}, bf16[17,256]{1,0:T(8,128)(2,1)S(1)}, u32[]{:S(2)}, u32[]{:S(2)}) collective-permute-start(bf16[17,256]{1,0:T(8,128)(2,1)S(1)} %get-tuple-element.161), channel_id=1, source_target_pairs={{8,0},{16,8},{24,16},{32,24},{40,32},{48,40},{56,48},{64,56},{72,6... | collective-permute-start | bytes 26120 | tf_op jit(solution)/shard_map/ppermute | solution.py:21
  41.4 19.6 %copy-start.1 = (f32[3]{0:T(128)S(1)}, f32[3]{0:T(128)}, u32[]{:S(2)}) copy-start(f32[3]{0:T(128)} %param.13) | copy-start | bytes 40
  79.9 79.2 %copy-start = (s32[64,256]{1,0:T(8,128)S(1)}, s32[64,256]{1,0:T(8,128)}, u32[]{:S(2)}) copy-start(s32[64,256]{1,0:T(8,128)} %param.11) | copy-start | bytes 196612
  80.9 212.7 %reduce-scatter.2.cloned.1.call-start = ((), (), s32[]{:S(2)}) async-start(), calls=%async_computation.2 | async-start | bytes 147456 | tf_op jit(solution)/shard_map/reduce_scatter | solution.py:130
  160.0 8.8 %collective-permute-start.2 = (bf16[6,17,256]{2,1,0:T(8,128)(2,1)S(1)}, bf16[6,17,256]{2,1,0:T(8,128)(2,1)S(1)}, u32[]{:S(2)}, u32[]{:S(2)}) collective-permute-start(bf16[6,17,256]{2,1,0:T(8,128)(2,1)S(1)} %get-tuple-element.158), channel_id=1, source_target_pairs={{0,8},{8,16},{16,24},{24,32},{32,40},{40,48},{48,56},{56,64},{64,7... | collective-permute-start | bytes 156680 | tf_op jit(solution)/shard_map/ppermute | solution.py:19
  162.0 8.6 %collective-permute-start.3 = (bf16[6,17,256]{2,1,0:T(8,128)(2,1)S(1)}, bf16[6,17,256]{2,1,0:T(8,128)(2,1)S(1)}, u32[]{:S(2)}, u32[]{:S(2)}) collective-permute-start(bf16[6,17,256]{2,1,0:T(8,128)(2,1)S(1)} %get-tuple-element.159), channel_id=1, source_target_pairs={{8,0},{16,8},{24,16},{32,24},{40,32},{48,40},{56,48},{64,56},{72,6... | collective-permute-start | bytes 156680 | tf_op jit(solution)/shard_map/ppermute | solution.py:21
Sparse Core Ops, SparseCore 0:
  81.0 77.9 all-reduce.40
  254.0 39.4 reduce-scatter.1
where the time goes:
time: 305 us; the launch traced here: 300 us
  waiting for transfers between devices  119 us (39%)
  local copies, waits for them, and re-layouts  94 us (31%)
  matrix products  42.1 us (14%)
  starting transfers between devices  22.7 us (7%)
  between operations  13.6 us (4%)
  loops' own time  4.64 us (2%)
  other arithmetic  4.34 us (1%)
    psum x1, waiting for transfers between devices, on_device(): intensity = lax.psum(partial_sum, 'kern')  77.6 us
    dot_general x8, local copies, waits for them, and re-layouts, adjoint_block(): lax.dot_general(piece, matrix, (((1,), (1,)), ((), ())), preferred_elemen...  44.3 us
    reduce_scatter x1, waiting for transfers between devices, on_device(): return lax.psum_scatter(local_grad, 'kern', scatter_dimension=1, tiled=True)  39.6 us
    convert_element_type x2, local copies, waits for them, and re-layouts, band_matrix(): return matrix.reshape(tap_count * span_cols, -1).astype(jnp.bfloat16)  33.5 us
    dot_general x4, matrix products, adjoint_block(): lax.dot_general(piece, matrix, (((1,), (1,)), ((), ())), preferred_elemen...  26.3 us
    ppermute x2, starting transfers between devices, extended_2(): lax.ppermute(head, axis, [((i + 1) % count, i) for i in range(ends)])  18.8 us
    dot_general x2, matrix products, forward_block(): jnp.dot(col_blocks.reshape(block_rows * block_count, tap_count * span_col...  9.74 us
  transfers between devices with their start and end apart: 6, of which 3 were waited for; matrix products, arithmetic and copies ran while one was open for 13% of the time, Pallas kernels for 0%

commit v1 on v0

v1 whole, which is shorter than its diff:
```python
import functools

import jax
import jax.numpy as jnp
from jax import lax
from jax.experimental import pallas as pl
from jax.experimental.pallas import tpu as pltpu
from jax.sharding import PartitionSpec as P

steepness = 10.0
threshold = 0.4

TAPS = 35
HALF = 17
PITCH = 48
FLAT = 1792
TAP_LANES = TAPS * PITCH
GROUP = 8
FIELD_BLOCKS = 9
OUT_BLOCKS = 4
PARTNERS = 8
LOCAL = 6
CHANNELS = PARTNERS * LOCAL
ROWS = 64
OWN_COLS = 32
WIDTH = 256
FIELD_ROWS = GROUP * CHANNELS
TAP_PITCH = 40
VMEM = 50 * 1024 * 1024


def prepare(levels_ref, jitter_ref, target_ref, kernels_ref, weight_ref,
            mask_ref, goal_ref, next_ref, prev_ref, taps_ref):
    kern = lax.axis_index("kern")
    first_col = kern * OWN_COLS

    def columns(whole, before):
        shift = lax.rem(WIDTH + before - first_col, WIDTH)
        rolled = pltpu.roll(whole, shift, 1)[:, :128]
        col = lax.broadcasted_iota(jnp.int32, (ROWS, 128), 1) + (first_col - before)
        return jnp.where((col >= 0) & (col < WIDTH), rolled, 0.0)

    logits = levels_ref[...].astype(jnp.float32) - 1.5 + jitter_ref[...]
    mask = (1.0 / (1.0 + jnp.exp(-logits))).astype(jnp.bfloat16).astype(jnp.float32)
    mask = columns(mask, 2 * HALF)
    goal = columns(target_ref[...].astype(jnp.float32), HALF)
    mask_ref[...] = mask
    goal_ref[...] = goal
    next_ref[...] = jnp.concatenate([mask[24:64], goal[40:64]], 0).astype(jnp.bfloat16)
    prev_ref[...] = jnp.concatenate([mask[0:40], goal[0:24]], 0).astype(jnp.bfloat16)

    taps = kernels_ref[...].astype(jnp.float32)
    gap = jnp.zeros((LOCAL, PITCH - TAPS), jnp.float32)
    pieces = []
    for i in range(TAPS):
        pieces += [taps[:, i, :], gap]
    row = lax.broadcasted_iota(jnp.int32, (LOCAL, 1), 0)
    weight = jnp.where(row < 2, weight_ref[0], jnp.where(row < 4, weight_ref[1], weight_ref[2]))
    high = weight.astype(jnp.bfloat16).astype(jnp.float32)
    middle = (weight - high).astype(jnp.bfloat16).astype(jnp.float32)
    low = weight - high - middle
    lane = lax.broadcasted_iota(jnp.int32, (LOCAL, FLAT - TAP_LANES), 1)
    tail = jnp.where(lane == 0, high, jnp.where(lane == 1, middle, jnp.where(lane == 2, low, 0.0)))
    flat = jnp.concatenate(pieces + [tail], 1).astype(jnp.bfloat16)
    for partner in range(PARTNERS):
        taps_ref[partner] = flat


def gradient(mask_ref, goal_ref, up_ref, down_ref, taps_ref, out_ref,
             flat_ref, turned_ref, band_ref, image_ref, adjoint_ref, back_ref):
    tile = lax.axis_index("tile")
    kern = lax.axis_index("kern")
    tiles = lax.axis_size("tile")
    up = up_ref[...].astype(jnp.float32)
    down = down_ref[...].astype(jnp.float32)

    line = lax.broadcasted_iota(jnp.int32, (16, 128), 0) + 88
    mask = mask_ref[...]

    def circle(first_up):
        mixed = jnp.where(line >= first_up, up[0:16], down[24:40])
        return jnp.concatenate([mask, down[0:24], mixed, up[16:40]], 0).T

    image_above = circle(94)
    image_below = circle(98)
    goal = jnp.concatenate(
        [goal_ref[...], down[40:64], jnp.zeros((16, 128), jnp.float32), up[40:64]], 0
    ).T

    for i in range(TAPS):
        source = image_above if i < HALF else image_below
        turned = pltpu.roll(source, (HALF - i) % 128, 1)
        even = turned[0:112].astype(jnp.bfloat16)
        odd = turned[8:104].astype(jnp.bfloat16)
        for b in range(FIELD_BLOCKS):
            piece = even[8 * b : 8 * b + PITCH] if b % 2 == 0 else odd[8 * b - 8 : 8 * b - 8 + PITCH]
            image_ref[PITCH * i : PITCH * (i + 1), 128 * b : 128 * (b + 1)] = piece
    image_ref[TAP_LANES:, :] = jnp.zeros((FLAT - TAP_LANES, 128 * FIELD_BLOCKS), jnp.bfloat16)

    for partner in range(PARTNERS):
        flat_ref[LOCAL * partner : LOCAL * (partner + 1), :] = taps_ref[partner].astype(jnp.float32)
    last = flat_ref[:, TAP_LANES : TAP_LANES + 3]
    weight = last[:, 0:1] + last[:, 1:2] + last[:, 2:3]
    lane = lax.broadcasted_iota(jnp.int32, (CHANNELS, FLAT), 1)
    flat = jnp.where(lane < TAP_LANES, flat_ref[...], 0.0)
    for d in range(GROUP):
        shifted = flat if d == 0 else pltpu.roll(flat, d, 1)
        band_ref[CHANNELS * d : CHANNELS * (d + 1), :] = shifted.astype(jnp.bfloat16)

    turned_ref[...] = jnp.concatenate([flat, jnp.zeros((128 - CHANNELS, FLAT), jnp.float32)], 0).T
    pieces = []
    for j in range(TAPS):
        pieces.append(turned_ref[pl.ds(TAPS - 1 - j, TAPS, stride=PITCH), :][:, :CHANNELS])
    pieces.append(jnp.zeros((TAPS, CHANNELS * (PITCH - TAPS)), jnp.float32))
    backward = jnp.concatenate(pieces, 1)
    backward = jnp.concatenate(
        [backward, jnp.zeros((TAP_PITCH - TAPS, CHANNELS * PITCH), jnp.float32)], 0
    )
    for d in range(GROUP):
        shifted = backward if d == 0 else pltpu.roll(backward, CHANNELS * d, 1)
        back_ref[TAP_PITCH * d : TAP_PITCH * (d + 1), :] = shifted.astype(jnp.bfloat16)

    at = lax.broadcasted_iota(jnp.int32, (GROUP, 128), 1)
    at = jnp.where(at < 96, at, at - 128)
    row_in_clip = at + tile * ROWS
    row_ok = (row_in_clip >= 0) & (row_in_clip < tiles * ROWS)
    step = lax.broadcasted_iota(jnp.int32, (GROUP, 128), 0)
    for b in range(FIELD_BLOCKS):
        fields = jnp.dot(
            band_ref[...], image_ref[:, 128 * b : 128 * (b + 1)], preferred_element_type=jnp.float32
        )
        fields = fields.reshape(GROUP, CHANNELS, 128)
        weighted = fields * weight[None]
        intensity = jnp.sum(weighted * fields, axis=1)
        resist = 1.0 / (1.0 + jnp.exp(-steepness * (intensity - threshold)))
        drive = 2.0 * (resist - goal[8 * b : 8 * b + 8]) * steepness * resist * (1.0 - resist)
        col = step + (8 * b - HALF + kern * OWN_COLS)
        drive = jnp.where(row_ok & (col >= 0) & (col < WIDTH), drive, 0.0)
        adjoint = (2.0 * weighted * drive[:, None, :]).astype(jnp.bfloat16).reshape(FIELD_ROWS, 128)
        if b < FIELD_BLOCKS - 1:
            adjoint_ref[FIELD_ROWS * b : FIELD_ROWS * (b + 1), 0:128] = adjoint
        if b > 0:
            adjoint_ref[FIELD_ROWS * (b - 1) : FIELD_ROWS * b, 128:256] = adjoint

    grads = []
    for n in range(OUT_BLOCKS // 2):
        spread = jnp.dot(
            back_ref[...],
            adjoint_ref[2 * FIELD_ROWS * n : 2 * FIELD_ROWS * n + CHANNELS * PITCH, :],
            preferred_element_type=jnp.float32,
        )
        for half in range(2):
            for d in range(GROUP):
                part = spread[TAP_PITCH * d : TAP_PITCH * (d + 1), 128 * half : 128 * (half + 1)]
                part = pltpu.roll(part, 0, 1, stride=1, stride_axis=0)
                grads.append(jnp.sum(part, axis=0, keepdims=True))
    grad = pltpu.roll(jnp.concatenate(grads, 0), 128 - HALF, 1)
    grad = jnp.concatenate([grad, jnp.zeros((128 - OWN_COLS, 128), jnp.float32)], 0).T
    out_ref[...] = grad[:ROWS, :OWN_COLS]


def on_device(levels, jitter, target, kernels, kernel_weight):
    vmem = pl.BlockSpec(memory_space=pltpu.VMEM)
    smem = pl.BlockSpec(memory_space=pltpu.SMEM)
    f32, bf16 = jnp.float32, jnp.bfloat16
    mask, goal, to_next, to_prev, taps = pl.pallas_call(
        prepare,
        out_shape=(
            jax.ShapeDtypeStruct((ROWS, 128), f32),
            jax.ShapeDtypeStruct((ROWS, 128), f32),
            jax.ShapeDtypeStruct((ROWS, 128), bf16),
            jax.ShapeDtypeStruct((ROWS, 128), bf16),
            jax.ShapeDtypeStruct((PARTNERS, LOCAL, FLAT), bf16),
        ),
        in_specs=[vmem, vmem, vmem, vmem, smem],
        out_specs=(vmem,) * 5,
        compiler_params=pltpu.CompilerParams(vmem_limit_bytes=VMEM),
        name="prepare",
    )(levels, jitter, target, kernels.reshape(LOCAL, TAPS, TAPS), kernel_weight)
    ends = lax.axis_size("tile") - 1
    all_taps = lax.all_to_all(taps, "kern", 0, 0)
    up = lax.ppermute(to_next, "tile", [(i, i + 1) for i in range(ends)])
    down = lax.ppermute(to_prev, "tile", [(i + 1, i) for i in range(ends)])
    return pl.pallas_call(
        gradient,
        out_shape=jax.ShapeDtypeStruct((ROWS, OWN_COLS), f32),
        in_specs=[vmem] * 5,
        out_specs=vmem,
        scratch_shapes=[
            pltpu.VMEM((CHANNELS, FLAT), f32),
            pltpu.VMEM((FLAT, 128), f32),
            pltpu.VMEM((FIELD_ROWS, FLAT), bf16),
            pltpu.VMEM((FLAT, 128 * FIELD_BLOCKS), bf16),
            pltpu.VMEM((FIELD_ROWS * (FIELD_BLOCKS - 1), 256), bf16),
            pltpu.VMEM((GROUP * TAP_PITCH, CHANNELS * PITCH), bf16),
        ],
        compiler_params=pltpu.CompilerParams(vmem_limit_bytes=VMEM),
        name="gradient",
    )(mask, goal, up, down, all_taps)


def solution(mesh):
    return jax.shard_map(
        on_device,
        mesh=mesh,
        in_specs=(
            P("tile", None),
            P("tile", None),
            P("tile", None),
            P("kern", None, None, None),
            P("kern"),
        ),
        out_specs=P("tile", "kern"),
        check_vma=False,
    )
```

time: 305 us -> 31.1 us (0.10); the launches traced: 300 us -> 30.8 us
  waiting for transfers between devices: 119 us -> 1.42 us
  local copies, waits for them, and re-layouts: 94 us -> 3.86 us
  matrix products: 42.1 us -> 0 us
  between operations: 13.6 us -> 0.05 us
  Pallas kernels: 0 us -> 6.37 us
  loops' own time: 4.64 us -> 0 us
  other arithmetic: 4.34 us -> 0 us
  starting transfers between devices: 22.7 us -> 19.1 us
    psum x1 -> x0, waiting for transfers between devices: 77.6 us -> none  [on_device(): intensity = lax.psum(partial_sum, 'kern')]
    dot_general x8 -> x0, local copies, waits for them, and re-layouts: 44.3 us -> none  [adjoint_block(): lax.dot_general(piece, matrix, (((1,), (1,)), ((), ())), preferred_elemen...]
    dot_general x7 -> x0, matrix products: 42.1 us -> none  [the longest x4 26.3 us: adjoint_block(): lax.dot_general(piece, matrix, (((1,), (1,)), ((), ())), preferred_elemen...]
    reduce_scatter x1 -> x0, waiting for transfers between devices: 39.6 us -> none  [on_device(): return lax.psum_scatter(local_grad, 'kern', scatter_dimension=1, tiled=True)]
    convert_element_type x2 -> x0, local copies, waits for them, and re-layouts: 33.5 us -> none  [band_matrix(): return matrix.reshape(tap_count * span_cols, -1).astype(jnp.bfloat16)]
    ppermute x4 -> x2, starting transfers between devices: 22.6 us -> 13.3 us  [the longest x1 11.4 us: on_device(): down = lax.ppermute(to_prev, 'tile', [(i + 1, i) for i in range(ends)])]
    pallas_call x0 -> x2, Pallas kernels: none -> 6.37 us  [the longest x1 5 us: on_device(): pl.pallas_call(gradient, out_shape=jax.ShapeDtypeStruct((ROWS, OWN_COLS),...]
    all_to_all x0 -> x1, starting transfers between devices: none -> 5.76 us  [on_device(): all_taps = lax.all_to_all(taps, 'kern', 0, 0)]
  transfers between devices with their start and end apart: 6 -> 3, of which waited for: 3 -> 1; matrix products, arithmetic and copies ran while one was open for 13% -> 0% of each run, Pallas kernels for 0% -> 0%
where the time goes in v1:
time: 31.1 us; the launch traced here: 30.8 us
  starting transfers between devices  19.1 us (61%)
  Pallas kernels  6.37 us (20%)
  local copies, waits for them, and re-layouts  3.86 us (12%)
  waiting for transfers between devices  1.42 us (5%)
    ppermute x1, starting transfers between devices, on_device(): down = lax.ppermute(to_prev, 'tile', [(i + 1, i) for i in range(ends)])  11.4 us
    all_to_all x1, starting transfers between devices, on_device(): all_taps = lax.all_to_all(taps, 'kern', 0, 0)  5.76 us
    pallas_call x1, Pallas kernels, on_device(): pl.pallas_call(gradient, out_shape=jax.ShapeDtypeStruct((ROWS, OWN_COLS),...  5 us
    unnamed x9, local copies, waits for them, and re-layouts  3.17 us
    ppermute x1, starting transfers between devices, on_device(): up = lax.ppermute(to_next, 'tile', [(i, i + 1) for i in range(ends)])  1.91 us
    ppermute x1, waiting for transfers between devices, on_device(): down = lax.ppermute(to_prev, 'tile', [(i + 1, i) for i in range(ends)])  1.41 us
    pallas_call x1, Pallas kernels, on_device(): pl.pallas_call(prepare, out_shape=(jax.ShapeDtypeStruct((ROWS, 128), f32)...  1.37 us
    pallas_call x1, local copies, waits for them, and re-layouts, on_device(): pl.pallas_call(gradient, out_shape=jax.ShapeDtypeStruct((ROWS, OWN_COLS),...  0.69 us
  transfers between devices with their start and end apart: 3, of which 1 were waited for; matrix products, arithmetic and copies ran while one was open for 0% of the time, Pallas kernels for 0%

profile of v1, /device:TPU:56, one launch (start us, length us, event | category | flops | bytes accessed | tf_op | source)
XLA Modules:
  0.0 30.8 jit_solution(10959534188787772662)
XLA Ops:
  0.0 0.0 copy-start
  0.0 0.9 %copy.6 = bf16[3,2,35,35]{3,2,1,0:T(8,128)(2,1)S(1)} copy(bf16[3,2,35,35]{3,1,2,0:T(2,128)(2,1)} %param.8) | data formatting | bytes 29400 | tf_op args[3]
  0.9 0.0 copy-start.3
  0.9 0.0 copy-done
  0.9 0.6 %copy-done.3 = f32[3]{0:T(128)S(1)} copy-done((f32[3]{0:T(128)S(1)}, f32[3]{0:T(128)}, u32[]{:S(2)}) %copy-start.3) | copy-done | bytes 36
  1.5 0.0 copy-start.1
  1.5 0.8 %copy-done.1 = f32[64,256]{1,0:T(8,128)S(1)} copy-done((f32[64,256]{1,0:T(8,128)S(1)}, f32[64,256]{1,0:T(8,128)}, u32[]{:S(2)}) %copy-start.1) | copy-done | bytes 65560
  2.4 0.0 copy-start.2
  2.4 0.8 %copy-done.2 = s32[64,256]{1,0:T(8,128)S(1)} copy-done((s32[64,256]{1,0:T(8,128)S(1)}, s32[64,256]{1,0:T(8,128)}, u32[]{:S(2)}) %copy-start.2) | copy-done | bytes 65560
  3.2 1.4 %prepare.1 = (f32[64,128]{1,0:T(8,128)S(1)}, f32[64,128]{1,0:T(8,128)S(1)}, bf16[64,128]{1,0:T(8,128)(2,1)S(1)}, bf16[64,128]{1,0:T(8,128)(2,1)S(1)}, bf16[8,6,1792]{2,1,0:T(8,128)(2,1)}) custom-call(s32[64,256]{1,0:T(8,128)S(1)} %copy-done, f32[64,256]{1,0:T(8,128)S(1)} %copy-done.1, s32[64,256]{1,0:T(8,128)S(1)} %copy-done.2, ...), custom_call_target="tpu_custom_call" | custom-call | tf_op jit(solution)/shard_map/prepare/pallas_call | solution.py:166
  4.6 5.8 %all-to-all-start = ((bf16[8,6,1792]{2,1,0:T(8,128)(2,1)}), bf16[8,6,1792]{2,1,0:T(8,128)(2,1)S(1)}, u32[]{:S(2)}, u32[]{:S(2)}) async-start(bf16[8,6,1792]{2,1,0:T(8,128)(2,1)} %get-tuple-element.14), calls=%async_computation | async-start | bytes 458752 | tf_op jit(solution)/shard_map/all_to_all | solution.py:181
  10.3 1.9 %collective-permute-start = (bf16[64,128]{1,0:T(8,128)(2,1)S(1)}, bf16[64,128]{1,0:T(8,128)(2,1)S(1)}, u32[]{:S(2)}, u32[]{:S(2)}) collective-permute-start(bf16[64,128]{1,0:T(8,128)(2,1)S(1)} %get-tuple-element.12), channel_id=1, source_target_pairs={{0,8},{8,16},{16,24},{24,32},{32,40},{40,48},{48,56},{56,64},{64,7... | collective-permute-start | bytes 49160 | tf_op jit(solution)/shard_map/ppermute | solution.py:182
  12.2 11.4 %collective-permute-start.1 = (bf16[64,128]{1,0:T(8,128)(2,1)S(1)}, bf16[64,128]{1,0:T(8,128)(2,1)S(1)}, u32[]{:S(2)}, u32[]{:S(2)}) collective-permute-start(bf16[64,128]{1,0:T(8,128)(2,1)S(1)} %get-tuple-element.13), channel_id=1, source_target_pairs={{8,0},{16,8},{24,16},{32,24},{40,32},{48,40},{56,48},{64,56},{72,6... | collective-permute-start | bytes 49160 | tf_op jit(solution)/shard_map/ppermute | solution.py:183
  23.6 0.0 collective-permute-done.up_ref
  23.7 1.4 %collective-permute-done.1.down_ref = bf16[64,128]{1,0:T(8,128)(2,1)S(1)} collective-permute-done((bf16[64,128]{1,0:T(8,128)(2,1)S(1)}, bf16[64,128]{1,0:T(8,128)(2,1)S(1)}, u32[]{:S(2)}, u32[]{:S(2)}) %collective-permute-start.1) | collective-permute-done | bytes 16416 | tf_op jit(solution)/shard_map/ppermute | solution.py:183
  25.1 0.0 all-to-all-done.taps_ref
  25.1 5.0 %gradient.1 = f32[64,32]{1,0:T(8,128)S(1)} custom-call(f32[64,128]{1,0:T(8,128)S(1)} %get-tuple-element.10.mask_ref, f32[64,128]{1,0:T(8,128)S(1)} %get-tuple-element.11.goal_ref, bf16[64,128]{1,0:T(8,128)(2,1)S(1)} %collective-permute-done.up_ref, bf16[64,128]{1,0:T(8,128)(2,1)S(1)} %collective-permute-done.1.down_ref, ...), custom_call_target="tpu_custom_call" | custom-call | tf_op jit(solution)/shard_map/gradient/pallas_call | solution.py:184
  30.1 0.7 %copy.7 = f32[64,32]{0,1:T(8,128)} copy(f32[64,32]{1,0:T(8,128)S(1)} %gradient.1) | data formatting | bytes 16384 | tf_op jit(solution)/shard_map/gradient/pallas_call | solution.py:184
Async XLA Ops:
  0.0 0.9 %copy-start = (s32[64,256]{1,0:T(8,128)S(1)}, s32[64,256]{1,0:T(8,128)}, u32[]{:S(2)}) copy-start(s32[64,256]{1,0:T(8,128)} %levels_ref.1) | copy-start | bytes 196612
  0.9 0.7 %copy-start.3 = (f32[3]{0:T(128)S(1)}, f32[3]{0:T(128)}, u32[]{:S(2)}) copy-start(f32[3]{0:T(128)} %weight_ref.1) | copy-start | bytes 40
  1.5 0.8 %copy-start.1 = (f32[64,256]{1,0:T(8,128)S(1)}, f32[64,256]{1,0:T(8,128)}, u32[]{:S(2)}) copy-start(f32[64,256]{1,0:T(8,128)} %jitter_ref.1) | copy-start | bytes 196612
  2.4 0.8 %copy-start.2 = (s32[64,256]{1,0:T(8,128)S(1)}, s32[64,256]{1,0:T(8,128)}, u32[]{:S(2)}) copy-start(s32[64,256]{1,0:T(8,128)} %target_ref.1) | copy-start | bytes 196612
  4.6 20.5 %all-to-all-start = ((bf16[8,6,1792]{2,1,0:T(8,128)(2,1)}), bf16[8,6,1792]{2,1,0:T(8,128)(2,1)S(1)}, u32[]{:S(2)}, u32[]{:S(2)}) async-start(bf16[8,6,1792]{2,1,0:T(8,128)(2,1)} %get-tuple-element.14), calls=%async_computation | async-start | bytes 458752 | tf_op jit(solution)/shard_map/all_to_all | solution.py:181
  10.3 13.3 %collective-permute-start = (bf16[64,128]{1,0:T(8,128)(2,1)S(1)}, bf16[64,128]{1,0:T(8,128)(2,1)S(1)}, u32[]{:S(2)}, u32[]{:S(2)}) collective-permute-start(bf16[64,128]{1,0:T(8,128)(2,1)S(1)} %get-tuple-element.12), channel_id=1, source_target_pairs={{0,8},{8,16},{16,24},{24,32},{32,40},{40,48},{48,56},{56,64},{64,7... | collective-permute-start | bytes 49160 | tf_op jit(solution)/shard_map/ppermute | solution.py:182
  12.2 12.8 %collective-permute-start.1 = (bf16[64,128]{1,0:T(8,128)(2,1)S(1)}, bf16[64,128]{1,0:T(8,128)(2,1)S(1)}, u32[]{:S(2)}, u32[]{:S(2)}) collective-permute-start(bf16[64,128]{1,0:T(8,128)(2,1)S(1)} %get-tuple-element.13), channel_id=1, source_target_pairs={{8,0},{16,8},{24,16},{32,24},{40,32},{48,40},{56,48},{64,56},{72,6... | collective-permute-start | bytes 49160 | tf_op jit(solution)/shard_map/ppermute | solution.py:183

commit v2 on v1

--- a/solution.py
+++ b/solution.py
@@ -29,8 +29,21 @@
 VMEM = 50 * 1024 * 1024
 
 
-def prepare(levels_ref, jitter_ref, target_ref, kernels_ref, weight_ref,
-            mask_ref, goal_ref, next_ref, prev_ref, taps_ref):
+def prepare(levels_hbm, jitter_hbm, target_hbm, kernels_hbm, weight_hbm,
+            mask_ref, goal_ref, next_ref, prev_ref, taps_ref,
+            levels_ref, jitter_ref, target_ref, kernels_ref, weight_ref, arrived):
+    copies = [
+        pltpu.make_async_copy(source, place, arrived.at[n])
+        for n, (source, place) in enumerate([
+            (levels_hbm, levels_ref),
+            (jitter_hbm, jitter_ref),
+            (target_hbm, target_ref),
+            (kernels_hbm, kernels_ref),
+            (weight_hbm, weight_ref),
+        ])
+    ]
+    for copy in copies:
+        copy.start()
     kern = lax.axis_index("kern")
     first_col = kern * OWN_COLS
 
@@ -40,6 +53,8 @@
         col = lax.broadcasted_iota(jnp.int32, (ROWS, 128), 1) + (first_col - before)
         return jnp.where((col >= 0) & (col < WIDTH), rolled, 0.0)
 
+    for copy in copies:
+        copy.wait()
     logits = levels_ref[...].astype(jnp.float32) - 1.5 + jitter_ref[...]
     mask = (1.0 / (1.0 + jnp.exp(-logits))).astype(jnp.bfloat16).astype(jnp.float32)
     mask = columns(mask, 2 * HALF)
@@ -53,7 +68,7 @@
     gap = jnp.zeros((LOCAL, PITCH - TAPS), jnp.float32)
     pieces = []
     for i in range(TAPS):
-        pieces += [taps[:, i, :], gap]
+        pieces += [jnp.concatenate([taps[k, i] for k in range(LOCAL // 2)], 0), gap]
     row = lax.broadcasted_iota(jnp.int32, (LOCAL, 1), 0)
     weight = jnp.where(row < 2, weight_ref[0], jnp.where(row < 4, weight_ref[1], weight_ref[2]))
     high = weight.astype(jnp.bfloat16).astype(jnp.float32)
@@ -66,8 +81,8 @@
         taps_ref[partner] = flat
 
 
-def gradient(mask_ref, goal_ref, up_ref, down_ref, taps_ref, out_ref,
-             flat_ref, turned_ref, band_ref, image_ref, adjoint_ref, back_ref):
+def gradient(mask_ref, goal_ref, up_ref, down_ref, taps_ref, out_hbm,
+             flat_ref, turned_ref, band_ref, image_ref, adjoint_ref, back_ref, out_ref, sent):
     tile = lax.axis_index("tile")
     kern = lax.axis_index("kern")
     tiles = lax.axis_size("tile")
@@ -125,22 +140,25 @@
     row_in_clip = at + tile * ROWS
     row_ok = (row_in_clip >= 0) & (row_in_clip < tiles * ROWS)
     step = lax.broadcasted_iota(jnp.int32, (GROUP, 128), 0)
-    for b in range(FIELD_BLOCKS):
-        fields = jnp.dot(
-            band_ref[...], image_ref[:, 128 * b : 128 * (b + 1)], preferred_element_type=jnp.float32
+    for first in range(0, FIELD_BLOCKS, 2):
+        count = min(2, FIELD_BLOCKS - first)
+        together = jnp.dot(
+            band_ref[...], image_ref[:, 128 * first : 128 * (first + count)], preferred_element_type=jnp.float32
         )
-        fields = fields.reshape(GROUP, CHANNELS, 128)
-        weighted = fields * weight[None]
-        intensity = jnp.sum(weighted * fields, axis=1)
-        resist = 1.0 / (1.0 + jnp.exp(-steepness * (intensity - threshold)))
-        drive = 2.0 * (resist - goal[8 * b : 8 * b + 8]) * steepness * resist * (1.0 - resist)
-        col = step + (8 * b - HALF + kern * OWN_COLS)
-        drive = jnp.where(row_ok & (col >= 0) & (col < WIDTH), drive, 0.0)
-        adjoint = (2.0 * weighted * drive[:, None, :]).astype(jnp.bfloat16).reshape(FIELD_ROWS, 128)
-        if b < FIELD_BLOCKS - 1:
-            adjoint_ref[FIELD_ROWS * b : FIELD_ROWS * (b + 1), 0:128] = adjoint
-        if b > 0:
-            adjoint_ref[FIELD_ROWS * (b - 1) : FIELD_ROWS * b, 128:256] = adjoint
+        for b in range(first, first + count):
+            fields = together[:, 128 * (b - first) : 128 * (b - first + 1)]
+            fields = fields.reshape(GROUP, CHANNELS, 128)
+            weighted = fields * weight[None]
+            intensity = jnp.sum(weighted * fields, axis=1)
+            resist = 1.0 / (1.0 + jnp.exp(-steepness * (intensity - threshold)))
+            drive = 2.0 * (resist - goal[8 * b : 8 * b + 8]) * steepness * resist * (1.0 - resist)
+            col = step + (8 * b - HALF + kern * OWN_COLS)
+            drive = jnp.where(row_ok & (col >= 0) & (col < WIDTH), drive, 0.0)
+            adjoint = (2.0 * weighted * drive[:, None, :]).astype(jnp.bfloat16).reshape(FIELD_ROWS, 128)
+            if b < FIELD_BLOCKS - 1:
+                adjoint_ref[FIELD_ROWS * b : FIELD_ROWS * (b + 1), 0:128] = adjoint
+            if b > 0:
+                adjoint_ref[FIELD_ROWS * (b - 1) : FIELD_ROWS * b, 128:256] = adjoint
 
     grads = []
     for n in range(OUT_BLOCKS // 2):
@@ -154,14 +172,15 @@
                 part = spread[TAP_PITCH * d : TAP_PITCH * (d + 1), 128 * half : 128 * (half + 1)]
                 part = pltpu.roll(part, 0, 1, stride=1, stride_axis=0)
                 grads.append(jnp.sum(part, axis=0, keepdims=True))
-    grad = pltpu.roll(jnp.concatenate(grads, 0), 128 - HALF, 1)
-    grad = jnp.concatenate([grad, jnp.zeros((128 - OWN_COLS, 128), jnp.float32)], 0).T
-    out_ref[...] = grad[:ROWS, :OWN_COLS]
+    out_ref[...] = pltpu.roll(jnp.concatenate(grads, 0), 128 - HALF, 1)[:, :ROWS]
+    copy = pltpu.make_async_copy(out_ref, out_hbm, sent)
+    copy.start()
+    copy.wait()
 
 
 def on_device(levels, jitter, target, kernels, kernel_weight):
     vmem = pl.BlockSpec(memory_space=pltpu.VMEM)
-    smem = pl.BlockSpec(memory_space=pltpu.SMEM)
+    hbm = pl.BlockSpec(memory_space=pltpu.HBM)
     f32, bf16 = jnp.float32, jnp.bfloat16
     mask, goal, to_next, to_prev, taps = pl.pallas_call(
         prepare,
@@ -172,20 +191,31 @@
             jax.ShapeDtypeStruct((ROWS, 128), bf16),
             jax.ShapeDtypeStruct((PARTNERS, LOCAL, FLAT), bf16),
         ),
-        in_specs=[vmem, vmem, vmem, vmem, smem],
+        in_specs=[hbm] * 5,
         out_specs=(vmem,) * 5,
+        scratch_shapes=[
+            pltpu.VMEM((ROWS, WIDTH), jnp.int32),
+            pltpu.VMEM((ROWS, WIDTH), f32),
+            pltpu.VMEM((ROWS, WIDTH), jnp.int32),
+            pltpu.VMEM((LOCAL // 2, TAPS, 2, TAPS), bf16),
+            pltpu.SMEM((LOCAL // 2,), f32),
+            pltpu.SemaphoreType.DMA((5,)),
+        ],
         compiler_params=pltpu.CompilerParams(vmem_limit_bytes=VMEM),
         name="prepare",
-    )(levels, jitter, target, kernels.reshape(LOCAL, TAPS, TAPS), kernel_weight)
+    )(*(
+        pltpu.with_memory_space_constraint(x, pltpu.HBM)
+        for x in (levels, jitter, target, kernels.transpose(0, 2, 1, 3), kernel_weight)
+    ))
     ends = lax.axis_size("tile") - 1
     all_taps = lax.all_to_all(taps, "kern", 0, 0)
     up = lax.ppermute(to_next, "tile", [(i, i + 1) for i in range(ends)])
     down = lax.ppermute(to_prev, "tile", [(i + 1, i) for i in range(ends)])
     return pl.pallas_call(
         gradient,
-        out_shape=jax.ShapeDtypeStruct((ROWS, OWN_COLS), f32),
+        out_shape=jax.ShapeDtypeStruct((OWN_COLS, ROWS), f32),
         in_specs=[vmem] * 5,
-        out_specs=vmem,
+        out_specs=hbm,
         scratch_shapes=[
             pltpu.VMEM((CHANNELS, FLAT), f32),
             pltpu.VMEM((FLAT, 128), f32),
@@ -193,10 +223,12 @@
             pltpu.VMEM((FLAT, 128 * FIELD_BLOCKS), bf16),
             pltpu.VMEM((FIELD_ROWS * (FIELD_BLOCKS - 1), 256), bf16),
             pltpu.VMEM((GROUP * TAP_PITCH, CHANNELS * PITCH), bf16),
+            pltpu.VMEM((OWN_COLS, ROWS), f32),
+            pltpu.SemaphoreType.DMA,
         ],
         compiler_params=pltpu.CompilerParams(vmem_limit_bytes=VMEM),
         name="gradient",
-    )(mask, goal, up, down, all_taps)
+    )(mask, goal, up, down, all_taps).T
 
 
 def solution(mesh):

time: 31.1 us -> 26.9 us (0.86)
  local copies, waits for them, and re-layouts: 3.86 us -> 0 us
    unnamed x9 -> x0, local copies, waits for them, and re-layouts: 3.17 us -> none
    pallas_call x1, Pallas kernels: 5 us -> 4.3 us  [on_device(): pl.pallas_call(gradient, out_shape=jax.ShapeDtypeStruct((OWN_COLS, ROWS),...]
    pallas_call x1 -> x0, local copies, waits for them, and re-layouts: 0.69 us -> none  [on_device(): pl.pallas_call(gradient, out_shape=jax.ShapeDtypeStruct((ROWS, OWN_COLS),...]
    pallas_call x1, Pallas kernels: 1.37 us -> 1.77 us  [on_device(): pl.pallas_call(prepare, out_shape=(jax.ShapeDtypeStruct((ROWS, 128), f32)...]
where the time goes in v2:
time: 26.9 us; the launch traced here: 26.6 us
  starting transfers between devices  19.1 us (71%)
  Pallas kernels  6.07 us (23%)
  waiting for transfers between devices  1.42 us (5%)
    ppermute x1, starting transfers between devices, on_device(): down = lax.ppermute(to_prev, 'tile', [(i + 1, i) for i in range(ends)])  11.4 us
    all_to_all x1, starting transfers between devices, on_device(): all_taps = lax.all_to_all(taps, 'kern', 0, 0)  5.77 us
    pallas_call x1, Pallas kernels, on_device(): pl.pallas_call(gradient, out_shape=jax.ShapeDtypeStruct((OWN_COLS, ROWS),...  4.3 us
    ppermute x1, starting transfers between devices, on_device(): up = lax.ppermute(to_next, 'tile', [(i, i + 1) for i in range(ends)])  1.91 us
    pallas_call x1, Pallas kernels, on_device(): pl.pallas_call(prepare, out_shape=(jax.ShapeDtypeStruct((ROWS, 128), f32)...  1.77 us
    ppermute x1, waiting for transfers between devices, on_device(): down = lax.ppermute(to_prev, 'tile', [(i + 1, i) for i in range(ends)])  1.41 us
  transfers between devices with their start and end apart: 3, of which 1 were waited for; matrix products, arithmetic and copies ran while one was open for 0% of the time, Pallas kernels for 0%

profile of v2, /device:TPU:56, one launch (start us, length us, event | category | flops | bytes accessed | tf_op | source)
XLA Modules:
  0.0 26.6 jit_solution(7166608778432400082)
XLA Ops:
  0.0 1.8 %prepare.1 = (f32[64,128]{1,0:T(8,128)S(1)}, f32[64,128]{1,0:T(8,128)S(1)}, bf16[64,128]{1,0:T(8,128)(2,1)S(1)}, bf16[64,128]{1,0:T(8,128)(2,1)S(1)}, bf16[8,6,1792]{2,1,0:T(8,128)(2,1)}) custom-call(s32[64,256]{1,0:T(8,128)} %levels_hbm.1, f32[64,256]{1,0:T(8,128)} %jitter_hbm.1, s32[64,256]{1,0:T(8,128)} %target_hbm.1, bf16[3,35,2,35]{3,2,1,0:T(2,128)(2,1)} %bitcast.2, ...), custom_call_target="tpu_custom_call" | custom-call | tf_op jit(solution)/shard_map/prepare/pallas_call | solution.py:185
  1.8 5.8 %all-to-all-start = ((bf16[8,6,1792]{2,1,0:T(8,128)(2,1)}), bf16[8,6,1792]{2,1,0:T(8,128)(2,1)S(1)}, u32[]{:S(2)}, u32[]{:S(2)}) async-start(bf16[8,6,1792]{2,1,0:T(8,128)(2,1)} %get-tuple-element.14), calls=%async_computation | async-start | bytes 458752 | tf_op jit(solution)/shard_map/all_to_all | solution.py:211
  7.5 1.9 %collective-permute-start = (bf16[64,128]{1,0:T(8,128)(2,1)S(1)}, bf16[64,128]{1,0:T(8,128)(2,1)S(1)}, u32[]{:S(2)}, u32[]{:S(2)}) collective-permute-start(bf16[64,128]{1,0:T(8,128)(2,1)S(1)} %get-tuple-element.12), channel_id=1, source_target_pairs={{0,8},{8,16},{16,24},{24,32},{32,40},{40,48},{48,56},{56,64},{64,7... | collective-permute-start | bytes 49160 | tf_op jit(solution)/shard_map/ppermute | solution.py:212
  9.5 11.4 %collective-permute-start.1 = (bf16[64,128]{1,0:T(8,128)(2,1)S(1)}, bf16[64,128]{1,0:T(8,128)(2,1)S(1)}, u32[]{:S(2)}, u32[]{:S(2)}) collective-permute-start(bf16[64,128]{1,0:T(8,128)(2,1)S(1)} %get-tuple-element.13), channel_id=1, source_target_pairs={{8,0},{16,8},{24,16},{32,24},{40,32},{48,40},{56,48},{64,56},{72,6... | collective-permute-start | bytes 49160 | tf_op jit(solution)/shard_map/ppermute | solution.py:213
  20.9 0.0 collective-permute-done.up_ref
  20.9 1.4 %collective-permute-done.1.down_ref = bf16[64,128]{1,0:T(8,128)(2,1)S(1)} collective-permute-done((bf16[64,128]{1,0:T(8,128)(2,1)S(1)}, bf16[64,128]{1,0:T(8,128)(2,1)S(1)}, u32[]{:S(2)}, u32[]{:S(2)}) %collective-permute-start.1) | collective-permute-done | bytes 16416 | tf_op jit(solution)/shard_map/ppermute | solution.py:213
  22.3 0.0 all-to-all-done.taps_ref
  22.3 4.3 %gradient.1 = f32[32,64]{1,0:T(8,128)} custom-call(f32[64,128]{1,0:T(8,128)S(1)} %get-tuple-element.10.mask_ref, f32[64,128]{1,0:T(8,128)S(1)} %get-tuple-element.11.goal_ref, bf16[64,128]{1,0:T(8,128)(2,1)S(1)} %collective-permute-done.up_ref, bf16[64,128]{1,0:T(8,128)(2,1)S(1)} %collective-permute-done.1.down_ref, ...), custom_call_target="tpu_custom_call" | custom-call | tf_op jit(solution)/shard_map/gradient/pallas_call | solution.py:214
Async XLA Ops:
  1.8 20.5 %all-to-all-start = ((bf16[8,6,1792]{2,1,0:T(8,128)(2,1)}), bf16[8,6,1792]{2,1,0:T(8,128)(2,1)S(1)}, u32[]{:S(2)}, u32[]{:S(2)}) async-start(bf16[8,6,1792]{2,1,0:T(8,128)(2,1)} %get-tuple-element.14), calls=%async_computation | async-start | bytes 458752 | tf_op jit(solution)/shard_map/all_to_all | solution.py:211
  7.5 13.3 %collective-permute-start = (bf16[64,128]{1,0:T(8,128)(2,1)S(1)}, bf16[64,128]{1,0:T(8,128)(2,1)S(1)}, u32[]{:S(2)}, u32[]{:S(2)}) collective-permute-start(bf16[64,128]{1,0:T(8,128)(2,1)S(1)} %get-tuple-element.12), channel_id=1, source_target_pairs={{0,8},{8,16},{16,24},{24,32},{32,40},{40,48},{48,56},{56,64},{64,7... | collective-permute-start | bytes 49160 | tf_op jit(solution)/shard_map/ppermute | solution.py:212
  9.5 12.8 %collective-permute-start.1 = (bf16[64,128]{1,0:T(8,128)(2,1)S(1)}, bf16[64,128]{1,0:T(8,128)(2,1)S(1)}, u32[]{:S(2)}, u32[]{:S(2)}) collective-permute-start(bf16[64,128]{1,0:T(8,128)(2,1)S(1)} %get-tuple-element.13), channel_id=1, source_target_pairs={{8,0},{16,8},{24,16},{32,24},{40,32},{48,40},{56,48},{64,56},{72,6... | collective-permute-start | bytes 49160 | tf_op jit(solution)/shard_map/ppermute | solution.py:213

commit v3 on v2

--- a/solution.py
+++ b/solution.py
@@ -22,6 +22,8 @@
 LOCAL = 6
 CHANNELS = PARTNERS * LOCAL
 ROWS = 64
+SHARE = 8
+HALF_FLAT = FLAT // 2
 OWN_COLS = 32
 WIDTH = 256
 FIELD_ROWS = GROUP * CHANNELS
@@ -30,8 +32,8 @@
 
 
 def prepare(levels_hbm, jitter_hbm, target_hbm, kernels_hbm, weight_hbm,
-            mask_ref, goal_ref, next_ref, prev_ref, taps_ref,
-            levels_ref, jitter_ref, target_ref, kernels_ref, weight_ref, arrived):
+            mask_ref, goal_ref, far_ref, message_ref,
+            levels_ref, jitter_ref, target_ref, kernels_ref, weight_ref, near_ref, arrived):
     copies = [
         pltpu.make_async_copy(source, place, arrived.at[n])
         for n, (source, place) in enumerate([
@@ -45,6 +47,7 @@
     for copy in copies:
         copy.start()
     kern = lax.axis_index("kern")
+    core = lax.axis_index("core")
     first_col = kern * OWN_COLS
 
     def columns(whole, before):
@@ -57,12 +60,26 @@
         copy.wait()
     logits = levels_ref[...].astype(jnp.float32) - 1.5 + jitter_ref[...]
     mask = (1.0 / (1.0 + jnp.exp(-logits))).astype(jnp.bfloat16).astype(jnp.float32)
-    mask = columns(mask, 2 * HALF)
-    goal = columns(target_ref[...].astype(jnp.float32), HALF)
-    mask_ref[...] = mask
-    goal_ref[...] = goal
-    next_ref[...] = jnp.concatenate([mask[24:64], goal[40:64]], 0).astype(jnp.bfloat16)
-    prev_ref[...] = jnp.concatenate([mask[0:40], goal[0:24]], 0).astype(jnp.bfloat16)
+    goal = target_ref[...].astype(jnp.float32)
+    own_mask = columns(mask, 2 * HALF)
+    own_goal = columns(goal, HALF)
+    mask_ref[...] = own_mask
+    goal_ref[...] = own_goal
+    odd = core == 1
+    far_mask = jnp.where(odd, own_mask[24:64], own_mask[0:40])
+    far_goal = jnp.where(odd, own_goal[40:64], own_goal[0:24])
+    far_ref[...] = jnp.concatenate([far_mask, far_goal], 0).astype(jnp.bfloat16)
+    near_ref[0:40] = jnp.where(odd, mask[0:40], mask[24:64])
+    near_goal = jnp.where(odd, goal[0:24], goal[40:64])
+    near_ref[40:64] = pltpu.roll(near_goal, WIDTH - HALF, 1)
+    share = near_ref[pl.ds(pl.multiple_of(kern * SHARE, SHARE), SHARE), :]
+    lane = lax.broadcasted_iota(jnp.int32, (SHARE, 128), 1)
+    shares = []
+    for partner in range(PARTNERS):
+        start = partner * OWN_COLS - 2 * HALF
+        rolled = pltpu.roll(share, (-start) % WIDTH, 1)[:, :128]
+        inside = (lane >= -start) & (lane < WIDTH - start)
+        shares.append(jnp.where(inside | (kern >= 40 // SHARE), rolled, 0.0).astype(jnp.bfloat16))
 
     taps = kernels_ref[...].astype(jnp.float32)
     gap = jnp.zeros((LOCAL, PITCH - TAPS), jnp.float32)
@@ -76,18 +93,27 @@
     low = weight - high - middle
     lane = lax.broadcasted_iota(jnp.int32, (LOCAL, FLAT - TAP_LANES), 1)
     tail = jnp.where(lane == 0, high, jnp.where(lane == 1, middle, jnp.where(lane == 2, low, 0.0)))
-    flat = jnp.concatenate(pieces + [tail], 1).astype(jnp.bfloat16)
+    flat = jnp.concatenate(pieces + [tail], 1)
+    part = jnp.where(odd, flat[:, HALF_FLAT:], flat[:, :HALF_FLAT])
+    part = jnp.concatenate([part, jnp.zeros((SHARE - LOCAL, HALF_FLAT), jnp.float32)], 0).astype(jnp.bfloat16)
     for partner in range(PARTNERS):
-        taps_ref[partner] = flat
-
-
-def gradient(mask_ref, goal_ref, up_ref, down_ref, taps_ref, out_hbm,
+        message = jnp.concatenate([part, shares[partner]], 1)
+        for to_core in range(2):
+            message_ref[PARTNERS * to_core + partner] = message
+
+
+def gradient(mask_ref, goal_ref, far_ref, message_ref, out_hbm,
              flat_ref, turned_ref, band_ref, image_ref, adjoint_ref, back_ref, out_ref, sent):
-    tile = lax.axis_index("tile")
+    core = lax.axis_index("core")
+    tile = lax.axis_index("pair") * 2 + core
+    tiles = lax.axis_size("pair") * 2
     kern = lax.axis_index("kern")
-    tiles = lax.axis_size("tile")
-    up = up_ref[...].astype(jnp.float32)
-    down = down_ref[...].astype(jnp.float32)
+    far = far_ref[...].astype(jnp.float32)
+    near = jnp.concatenate(
+        [message_ref[(1 - core) * PARTNERS + k, :, HALF_FLAT:].astype(jnp.float32) for k in range(PARTNERS)], 0
+    )
+    up = jnp.where(core == 1, near, far)
+    down = jnp.where(core == 1, far, near)
 
     line = lax.broadcasted_iota(jnp.int32, (16, 128), 0) + 88
     mask = mask_ref[...]
@@ -113,7 +139,9 @@
     image_ref[TAP_LANES:, :] = jnp.zeros((FLAT - TAP_LANES, 128 * FIELD_BLOCKS), jnp.bfloat16)
 
     for partner in range(PARTNERS):
-        flat_ref[LOCAL * partner : LOCAL * (partner + 1), :] = taps_ref[partner].astype(jnp.float32)
+        for half in range(2):
+            part = message_ref[PARTNERS * half + partner, :, :HALF_FLAT].astype(jnp.float32)
+            flat_ref[LOCAL * partner : LOCAL * (partner + 1), HALF_FLAT * half : HALF_FLAT * (half + 1)] = part[:LOCAL]
     last = flat_ref[:, TAP_LANES : TAP_LANES + 3]
     weight = last[:, 0:1] + last[:, 1:2] + last[:, 2:3]
     lane = lax.broadcasted_iota(jnp.int32, (CHANNELS, FLAT), 1)
@@ -182,23 +210,23 @@
     vmem = pl.BlockSpec(memory_space=pltpu.VMEM)
     hbm = pl.BlockSpec(memory_space=pltpu.HBM)
     f32, bf16 = jnp.float32, jnp.bfloat16
-    mask, goal, to_next, to_prev, taps = pl.pallas_call(
+    mask, goal, to_far, message = pl.pallas_call(
         prepare,
         out_shape=(
             jax.ShapeDtypeStruct((ROWS, 128), f32),
             jax.ShapeDtypeStruct((ROWS, 128), f32),
             jax.ShapeDtypeStruct((ROWS, 128), bf16),
-            jax.ShapeDtypeStruct((ROWS, 128), bf16),
-            jax.ShapeDtypeStruct((PARTNERS, LOCAL, FLAT), bf16),
+            jax.ShapeDtypeStruct((2 * PARTNERS, SHARE, HALF_FLAT + 128), bf16),
         ),
         in_specs=[hbm] * 5,
-        out_specs=(vmem,) * 5,
+        out_specs=(vmem,) * 4,
         scratch_shapes=[
             pltpu.VMEM((ROWS, WIDTH), jnp.int32),
             pltpu.VMEM((ROWS, WIDTH), f32),
             pltpu.VMEM((ROWS, WIDTH), jnp.int32),
             pltpu.VMEM((LOCAL // 2, TAPS, 2, TAPS), bf16),
             pltpu.SMEM((LOCAL // 2,), f32),
+            pltpu.VMEM((ROWS, WIDTH), f32),
             pltpu.SemaphoreType.DMA((5,)),
         ],
         compiler_params=pltpu.CompilerParams(vmem_limit_bytes=VMEM),
@@ -207,14 +235,14 @@
         pltpu.with_memory_space_constraint(x, pltpu.HBM)
         for x in (levels, jitter, target, kernels.transpose(0, 2, 1, 3), kernel_weight)
     ))
-    ends = lax.axis_size("tile") - 1
-    all_taps = lax.all_to_all(taps, "kern", 0, 0)
-    up = lax.ppermute(to_next, "tile", [(i, i + 1) for i in range(ends)])
-    down = lax.ppermute(to_prev, "tile", [(i + 1, i) for i in range(ends)])
+    pairs = lax.axis_size("pair")
+    messages = lax.all_to_all(message, ("core", "kern"), 0, 0)
+    meet = [(2 * p + 1, 2 * p + 2) for p in range(pairs - 1)]
+    far = lax.ppermute(to_far, ("pair", "core"), meet + [(b, a) for a, b in meet])
     return pl.pallas_call(
         gradient,
         out_shape=jax.ShapeDtypeStruct((OWN_COLS, ROWS), f32),
-        in_specs=[vmem] * 5,
+        in_specs=[vmem] * 4,
         out_specs=hbm,
         scratch_shapes=[
             pltpu.VMEM((CHANNELS, FLAT), f32),
@@ -228,20 +256,17 @@
         ],
         compiler_params=pltpu.CompilerParams(vmem_limit_bytes=VMEM),
         name="gradient",
-    )(mask, goal, up, down, all_taps).T
+    )(mask, goal, far, messages).T
 
 
 def solution(mesh):
+    tiles, partners = mesh.devices.shape
+    mesh = jax.sharding.Mesh(mesh.devices.reshape(tiles // 2, 2, partners), ("pair", "core", "kern"))
+    rows = P(("pair", "core"), None)
     return jax.shard_map(
         on_device,
         mesh=mesh,
-        in_specs=(
-            P("tile", None),
-            P("tile", None),
-            P("tile", None),
-            P("kern", None, None, None),
-            P("kern"),
-        ),
-        out_specs=P("tile", "kern"),
+        in_specs=(rows, rows, rows, P("kern", None, None, None), P("kern")),
+        out_specs=P(("pair", "core"), "kern"),
         check_vma=False,
     )

time: 26.9 us -> 26.1 us (0.970)
  starting transfers between devices: 19.1 us -> 18 us
    ppermute x2 -> x1, starting transfers between devices: 13.3 us -> 12.3 us  [on_device(): lax.ppermute(to_far, ('pair', 'core'), meet + [(b, a) for a, b in meet])]
    ppermute x2 -> x1, waiting for transfers between devices: 1.41 us -> 1.42 us  [on_device(): lax.ppermute(to_far, ('pair', 'core'), meet + [(b, a) for a, b in meet])]
  transfers between devices with their start and end apart: 3 -> 2, of which waited for: 1 -> 1; matrix products, arithmetic and copies ran while one was open for 0% -> 0% of each run, Pallas kernels for 0% -> 0%
where the time goes in v3:
time: 26.1 us; the launch traced here: 25.6 us
  starting transfers between devices  18 us (69%)
  Pallas kernels  6.1 us (23%)
  waiting for transfers between devices  1.42 us (5%)
    ppermute x1, starting transfers between devices, on_device(): lax.ppermute(to_far, ('pair', 'core'), meet + [(b, a) for a, b in meet])  12.3 us
    all_to_all x1, starting transfers between devices, on_device(): messages = lax.all_to_all(message, ('core', 'kern'), 0, 0)  5.79 us
    pallas_call x1, Pallas kernels, on_device(): pl.pallas_call(gradient, out_shape=jax.ShapeDtypeStruct((OWN_COLS, ROWS),...  4.3 us
    pallas_call x1, Pallas kernels, on_device(): pl.pallas_call(prepare, out_shape=(jax.ShapeDtypeStruct((ROWS, 128), f32)...  1.8 us
    ppermute x1, waiting for transfers between devices, on_device(): lax.ppermute(to_far, ('pair', 'core'), meet + [(b, a) for a, b in meet])  1.42 us
  transfers between devices with their start and end apart: 2, of which 1 were waited for; matrix products, arithmetic and copies ran while one was open for 0% of the time, Pallas kernels for 0%

profile of v3, /device:TPU:56, one launch (start us, length us, event | category | flops | bytes accessed | tf_op | source)
XLA Modules:
  0.0 25.6 jit_solution(412472901089073041)
XLA Ops:
  0.0 1.8 %prepare.1 = (f32[64,128]{1,0:T(8,128)S(1)}, f32[64,128]{1,0:T(8,128)S(1)}, bf16[64,128]{1,0:T(8,128)(2,1)S(1)}, bf16[16,8,1024]{2,1,0:T(8,128)(2,1)}) custom-call(s32[64,256]{1,0:T(8,128)} %levels_hbm.1, f32[64,256]{1,0:T(8,128)} %jitter_hbm.1, s32[64,256]{1,0:T(8,128)} %target_hbm.1, bf16[3,35,2,35]{3,2,1,0:T(2,128)(2,1)} %bitcast.2, f32[3]{0:T(128)} %weight_hbm.1), custom_call_target="tpu_custom_call" | custom-call | tf_op jit(solution)/shard_map/prepare/pallas_call | solution.py:213
  1.8 5.8 %all-to-all-start = ((bf16[16,8,1024]{2,1,0:T(8,128)(2,1)}), bf16[16,8,1024]{2,1,0:T(8,128)(2,1)S(1)}, u32[]{:S(2)}, u32[]{:S(2)}) async-start(bf16[16,8,1024]{2,1,0:T(8,128)(2,1)} %get-tuple-element.12), calls=%async_computation | async-start | bytes 524288 | tf_op jit(solution)/shard_map/all_to_all | solution.py:239
  7.6 12.3 %collective-permute-start = (bf16[64,128]{1,0:T(8,128)(2,1)S(1)}, bf16[64,128]{1,0:T(8,128)(2,1)S(1)}, u32[]{:S(2)}, u32[]{:S(2)}) collective-permute-start(bf16[64,128]{1,0:T(8,128)(2,1)S(1)} %get-tuple-element.11), channel_id=1, source_target_pairs={{8,16},{24,32},{40,48},{56,64},{72,80},{88,96},{104,112},{120,128}... | collective-permute-start | bytes 49160 | tf_op jit(solution)/shard_map/ppermute | solution.py:241
  19.9 1.4 %collective-permute-done.far_ref = bf16[64,128]{1,0:T(8,128)(2,1)S(1)} collective-permute-done((bf16[64,128]{1,0:T(8,128)(2,1)S(1)}, bf16[64,128]{1,0:T(8,128)(2,1)S(1)}, u32[]{:S(2)}, u32[]{:S(2)}) %collective-permute-start) | collective-permute-done | bytes 16416 | tf_op jit(solution)/shard_map/ppermute | solution.py:241
  21.3 0.0 all-to-all-done.message_ref
  21.3 4.3 %gradient.1 = f32[32,64]{1,0:T(8,128)} custom-call(f32[64,128]{1,0:T(8,128)S(1)} %get-tuple-element.9.mask_ref, f32[64,128]{1,0:T(8,128)S(1)} %get-tuple-element.10.goal_ref, bf16[64,128]{1,0:T(8,128)(2,1)S(1)} %collective-permute-done.far_ref, bf16[16,8,1024]{2,1,0:T(8,128)(2,1)S(1)} %all-to-all-done.message_ref), custom_call_target="tpu_custom_call" | custom-call | tf_op jit(solution)/shard_map/gradient/pallas_call | solution.py:242
Async XLA Ops:
  1.8 19.5 %all-to-all-start = ((bf16[16,8,1024]{2,1,0:T(8,128)(2,1)}), bf16[16,8,1024]{2,1,0:T(8,128)(2,1)S(1)}, u32[]{:S(2)}, u32[]{:S(2)}) async-start(bf16[16,8,1024]{2,1,0:T(8,128)(2,1)} %get-tuple-element.12), calls=%async_computation | async-start | bytes 524288 | tf_op jit(solution)/shard_map/all_to_all | solution.py:239
  7.6 13.7 %collective-permute-start = (bf16[64,128]{1,0:T(8,128)(2,1)S(1)}, bf16[64,128]{1,0:T(8,128)(2,1)S(1)}, u32[]{:S(2)}, u32[]{:S(2)}) collective-permute-start(bf16[64,128]{1,0:T(8,128)(2,1)S(1)} %get-tuple-element.11), channel_id=1, source_target_pairs={{8,16},{24,32},{40,48},{56,64},{72,80},{88,96},{104,112},{120,128}... | collective-permute-start | bytes 49160 | tf_op jit(solution)/shard_map/ppermute | solution.py:241

commit v4 on v3

--- a/solution.py
+++ b/solution.py
@@ -12,11 +12,13 @@
 
 TAPS = 35
 HALF = 17
+OWN_COLS = 32
 PITCH = 48
 FLAT = 1792
 TAP_LANES = TAPS * PITCH
 GROUP = 8
 FIELD_BLOCKS = 9
+FIELD_COLS = OWN_COLS + 2 * HALF
 OUT_BLOCKS = 4
 PARTNERS = 8
 LOCAL = 6
@@ -24,10 +26,10 @@
 ROWS = 64
 SHARE = 8
 HALF_FLAT = FLAT // 2
-OWN_COLS = 32
 WIDTH = 256
 FIELD_ROWS = GROUP * CHANNELS
 TAP_PITCH = 40
+DEPTH = 2048
 VMEM = 50 * 1024 * 1024
 
 
@@ -103,7 +105,7 @@
 
 
 def gradient(mask_ref, goal_ref, far_ref, message_ref, out_hbm,
-             flat_ref, turned_ref, band_ref, image_ref, adjoint_ref, back_ref, out_ref, sent):
+             flat_ref, turned_ref, band_ref, even_ref, odd_ref, adjoint_ref, back_ref, out_ref, sent):
     core = lax.axis_index("core")
     tile = lax.axis_index("pair") * 2 + core
     tiles = lax.axis_size("pair") * 2
@@ -131,12 +133,8 @@
     for i in range(TAPS):
         source = image_above if i < HALF else image_below
         turned = pltpu.roll(source, (HALF - i) % 128, 1)
-        even = turned[0:112].astype(jnp.bfloat16)
-        odd = turned[8:104].astype(jnp.bfloat16)
-        for b in range(FIELD_BLOCKS):
-            piece = even[8 * b : 8 * b + PITCH] if b % 2 == 0 else odd[8 * b - 8 : 8 * b - 8 + PITCH]
-            image_ref[PITCH * i : PITCH * (i + 1), 128 * b : 128 * (b + 1)] = piece
-    image_ref[TAP_LANES:, :] = jnp.zeros((FLAT - TAP_LANES, 128 * FIELD_BLOCKS), jnp.bfloat16)
+        even_ref[i] = turned[0:112].astype(jnp.bfloat16)
+        odd_ref[i] = turned[8:104].astype(jnp.bfloat16)
 
     for partner in range(PARTNERS):
         for half in range(2):
@@ -170,19 +168,28 @@
     step = lax.broadcasted_iota(jnp.int32, (GROUP, 128), 0)
     for first in range(0, FIELD_BLOCKS, 2):
         count = min(2, FIELD_BLOCKS - first)
+        groups = min(GROUP, FIELD_COLS - GROUP * first)
         together = jnp.dot(
-            band_ref[...], image_ref[:, 128 * first : 128 * (first + count)], preferred_element_type=jnp.float32
+            band_ref[: CHANNELS * groups, :TAP_LANES],
+            jnp.concatenate([
+                (even_ref if b % 2 == 0 else odd_ref)[:, 16 * (b // 2) : 16 * (b // 2) + PITCH, :].reshape(TAP_LANES, 128)
+                for b in range(first, first + count)
+            ], 1),
+            preferred_element_type=jnp.float32,
         )
         for b in range(first, first + count):
             fields = together[:, 128 * (b - first) : 128 * (b - first + 1)]
-            fields = fields.reshape(GROUP, CHANNELS, 128)
+            fields = fields.reshape(groups, CHANNELS, 128)
             weighted = fields * weight[None]
             intensity = jnp.sum(weighted * fields, axis=1)
             resist = 1.0 / (1.0 + jnp.exp(-steepness * (intensity - threshold)))
-            drive = 2.0 * (resist - goal[8 * b : 8 * b + 8]) * steepness * resist * (1.0 - resist)
-            col = step + (8 * b - HALF + kern * OWN_COLS)
-            drive = jnp.where(row_ok & (col >= 0) & (col < WIDTH), drive, 0.0)
-            adjoint = (2.0 * weighted * drive[:, None, :]).astype(jnp.bfloat16).reshape(FIELD_ROWS, 128)
+            drive = 2.0 * (resist - goal[8 * b : 8 * b + groups]) * steepness * resist * (1.0 - resist)
+            col = step[:groups] + (8 * b - HALF + kern * OWN_COLS)
+            drive = jnp.where(row_ok[:groups] & (col >= 0) & (col < WIDTH), drive, 0.0)
+            adjoint = (2.0 * weighted * drive[:, None, :]).astype(jnp.bfloat16).reshape(CHANNELS * groups, 128)
+            if groups < GROUP:
+                rest = jnp.zeros((FIELD_ROWS - CHANNELS * groups, 128), jnp.bfloat16)
+                adjoint = jnp.concatenate([adjoint, rest], 0)
             if b < FIELD_BLOCKS - 1:
                 adjoint_ref[FIELD_ROWS * b : FIELD_ROWS * (b + 1), 0:128] = adjoint
             if b > 0:
@@ -191,8 +198,8 @@
     grads = []
     for n in range(OUT_BLOCKS // 2):
         spread = jnp.dot(
-            back_ref[...],
-            adjoint_ref[2 * FIELD_ROWS * n : 2 * FIELD_ROWS * n + CHANNELS * PITCH, :],
+            back_ref[:, :DEPTH],
+            adjoint_ref[2 * FIELD_ROWS * n : 2 * FIELD_ROWS * n + DEPTH, :],
             preferred_element_type=jnp.float32,
         )
         for half in range(2):
@@ -248,7 +255,8 @@
             pltpu.VMEM((CHANNELS, FLAT), f32),
             pltpu.VMEM((FLAT, 128), f32),
             pltpu.VMEM((FIELD_ROWS, FLAT), bf16),
-            pltpu.VMEM((FLAT, 128 * FIELD_BLOCKS), bf16),
+            pltpu.VMEM((TAPS, 112, 128), bf16),
+            pltpu.VMEM((TAPS, 96, 128), bf16),
             pltpu.VMEM((FIELD_ROWS * (FIELD_BLOCKS - 1), 256), bf16),
             pltpu.VMEM((GROUP * TAP_PITCH, CHANNELS * PITCH), bf16),
             pltpu.VMEM((OWN_COLS, ROWS), f32),

time: 26.1 us -> 25.5 us (0.977)
  Pallas kernels: 6.1 us -> 5.51 us
    pallas_call x1, Pallas kernels: 4.3 us -> 3.71 us  [on_device(): pl.pallas_call(gradient, out_shape=jax.ShapeDtypeStruct((OWN_COLS, ROWS),...]
where the time goes in v4:
time: 25.5 us; the launch traced here: 25 us
  starting transfers between devices  18 us (71%)
  Pallas kernels  5.51 us (22%)
  waiting for transfers between devices  1.42 us (6%)
    ppermute x1, starting transfers between devices, on_device(): lax.ppermute(to_far, ('pair', 'core'), meet + [(b, a) for a, b in meet])  12.3 us
    all_to_all x1, starting transfers between devices, on_device(): messages = lax.all_to_all(message, ('core', 'kern'), 0, 0)  5.79 us
    pallas_call x1, Pallas kernels, on_device(): pl.pallas_call(gradient, out_shape=jax.ShapeDtypeStruct((OWN_COLS, ROWS),...  3.71 us
    pallas_call x1, Pallas kernels, on_device(): pl.pallas_call(prepare, out_shape=(jax.ShapeDtypeStruct((ROWS, 128), f32)...  1.8 us
    ppermute x1, waiting for transfers between devices, on_device(): lax.ppermute(to_far, ('pair', 'core'), meet + [(b, a) for a, b in meet])  1.42 us
  transfers between devices with their start and end apart: 2, of which 1 were waited for; matrix products, arithmetic and copies ran while one was open for 0% of the time, Pallas kernels for 0%

profile of v4, /device:TPU:56, one launch (start us, length us, event | category | flops | bytes accessed | tf_op | source)
XLA Modules:
  0.0 25.0 jit_solution(7220618288361689577)
XLA Ops:
  0.0 1.8 %prepare.1 = (f32[64,128]{1,0:T(8,128)S(1)}, f32[64,128]{1,0:T(8,128)S(1)}, bf16[64,128]{1,0:T(8,128)(2,1)S(1)}, bf16[16,8,1024]{2,1,0:T(8,128)(2,1)}) custom-call(s32[64,256]{1,0:T(8,128)} %levels_hbm.1, f32[64,256]{1,0:T(8,128)} %jitter_hbm.1, s32[64,256]{1,0:T(8,128)} %target_hbm.1, bf16[3,35,2,35]{3,2,1,0:T(2,128)(2,1)} %bitcast.2, f32[3]{0:T(128)} %weight_hbm.1), custom_call_target="tpu_custom_call" | custom-call | tf_op jit(solution)/shard_map/prepare/pallas_call | solution.py:220
  1.8 5.8 %all-to-all-start = ((bf16[16,8,1024]{2,1,0:T(8,128)(2,1)}), bf16[16,8,1024]{2,1,0:T(8,128)(2,1)S(1)}, u32[]{:S(2)}, u32[]{:S(2)}) async-start(bf16[16,8,1024]{2,1,0:T(8,128)(2,1)} %get-tuple-element.12), calls=%async_computation | async-start | bytes 524288 | tf_op jit(solution)/shard_map/all_to_all | solution.py:246
  7.6 12.3 %collective-permute-start = (bf16[64,128]{1,0:T(8,128)(2,1)S(1)}, bf16[64,128]{1,0:T(8,128)(2,1)S(1)}, u32[]{:S(2)}, u32[]{:S(2)}) collective-permute-start(bf16[64,128]{1,0:T(8,128)(2,1)S(1)} %get-tuple-element.11), channel_id=1, source_target_pairs={{8,16},{24,32},{40,48},{56,64},{72,80},{88,96},{104,112},{120,128}... | collective-permute-start | bytes 49160 | tf_op jit(solution)/shard_map/ppermute | solution.py:248
  19.9 1.4 %collective-permute-done.far_ref = bf16[64,128]{1,0:T(8,128)(2,1)S(1)} collective-permute-done((bf16[64,128]{1,0:T(8,128)(2,1)S(1)}, bf16[64,128]{1,0:T(8,128)(2,1)S(1)}, u32[]{:S(2)}, u32[]{:S(2)}) %collective-permute-start) | collective-permute-done | bytes 16416 | tf_op jit(solution)/shard_map/ppermute | solution.py:248
  21.3 0.0 all-to-all-done.message_ref
  21.3 3.7 %gradient.1 = f32[32,64]{1,0:T(8,128)} custom-call(f32[64,128]{1,0:T(8,128)S(1)} %get-tuple-element.9.mask_ref, f32[64,128]{1,0:T(8,128)S(1)} %get-tuple-element.10.goal_ref, bf16[64,128]{1,0:T(8,128)(2,1)S(1)} %collective-permute-done.far_ref, bf16[16,8,1024]{2,1,0:T(8,128)(2,1)S(1)} %all-to-all-done.message_ref), custom_call_target="tpu_custom_call" | custom-call | tf_op jit(solution)/shard_map/gradient/pallas_call | solution.py:249
Async XLA Ops:
  1.8 19.5 %all-to-all-start = ((bf16[16,8,1024]{2,1,0:T(8,128)(2,1)}), bf16[16,8,1024]{2,1,0:T(8,128)(2,1)S(1)}, u32[]{:S(2)}, u32[]{:S(2)}) async-start(bf16[16,8,1024]{2,1,0:T(8,128)(2,1)} %get-tuple-element.12), calls=%async_computation | async-start | bytes 524288 | tf_op jit(solution)/shard_map/all_to_all | solution.py:246
  7.6 13.7 %collective-permute-start = (bf16[64,128]{1,0:T(8,128)(2,1)S(1)}, bf16[64,128]{1,0:T(8,128)(2,1)S(1)}, u32[]{:S(2)}, u32[]{:S(2)}) collective-permute-start(bf16[64,128]{1,0:T(8,128)(2,1)S(1)} %get-tuple-element.11), channel_id=1, source_target_pairs={{8,16},{24,32},{40,48},{56,64},{72,80},{88,96},{104,112},{120,128}... | collective-permute-start | bytes 49160 | tf_op jit(solution)/shard_map/ppermute | solution.py:248

commit v5 on v4

--- a/solution.py
+++ b/solution.py
@@ -24,6 +24,9 @@
 LOCAL = 6
 CHANNELS = PARTNERS * LOCAL
 ROWS = 64
+RUN = 16
+RELAYED = (32, 48)
+LATE_COST = 33 * 10**8
 SHARE = 8
 HALF_FLAT = FLAT // 2
 WIDTH = 256
@@ -104,13 +107,21 @@
             message_ref[PARTNERS * to_core + partner] = message
 
 
+def either(far_ref, late_ref, passed_ref, rows_ref):
+    tile = lax.axis_index("pair") * 2 + lax.axis_index("core")
+    far = far_ref[...].astype(jnp.float32)
+    for start in RELAYED:
+        far = jnp.where(tile == start + RUN - 1, 0.0, far)
+    rows_ref[...] = far + late_ref[...].astype(jnp.float32) + passed_ref[...].astype(jnp.float32)
+
+
 def gradient(mask_ref, goal_ref, far_ref, message_ref, out_hbm,
              flat_ref, turned_ref, band_ref, even_ref, odd_ref, adjoint_ref, back_ref, out_ref, sent):
     core = lax.axis_index("core")
     tile = lax.axis_index("pair") * 2 + core
     tiles = lax.axis_size("pair") * 2
     kern = lax.axis_index("kern")
-    far = far_ref[...].astype(jnp.float32)
+    far = far_ref[...]
     near = jnp.concatenate(
         [message_ref[(1 - core) * PARTNERS + k, :, HALF_FLAT:].astype(jnp.float32) for k in range(PARTNERS)], 0
     )
@@ -242,10 +253,26 @@
         pltpu.with_memory_space_constraint(x, pltpu.HBM)
         for x in (levels, jitter, target, kernels.transpose(0, 2, 1, 3), kernel_weight)
     ))
-    pairs = lax.axis_size("pair")
+    tiles = lax.axis_size("pair") * 2
+    axes = ("pair", "core")
+    starts = range(RUN, tiles, RUN)
+    late = lax.ppermute(to_far, axes, [(t - 1, t) for t in starts])
     messages = lax.all_to_all(message, ("core", "kern"), 0, 0)
-    meet = [(2 * p + 1, 2 * p + 2) for p in range(pairs - 1)]
-    far = lax.ppermute(to_far, ("pair", "core"), meet + [(b, a) for a, b in meet])
+    meet = [(t, t + 1) for t in range(1, tiles - 1, 2)]
+    moves = [(a, b) for a, b in meet if b not in starts]
+    moves += [(b, a) for a, b in meet if b not in RELAYED] + [(t, t + RUN - 1) for t in RELAYED]
+    ends = lax.axis_index(axes) % RUN == RUN - 1
+    far = lax.ppermute(jnp.where(ends, late, to_far), axes, moves)
+    passed = lax.ppermute(far, axes, [(t + RUN - 1, t - 1) for t in RELAYED])
+    far = pl.pallas_call(
+        either,
+        out_shape=jax.ShapeDtypeStruct((ROWS, 128), f32),
+        in_specs=[vmem] * 3,
+        out_specs=vmem,
+        compiler_params=pltpu.CompilerParams(vmem_limit_bytes=2**21),
+        cost_estimate=pl.CostEstimate(flops=LATE_COST, bytes_accessed=2**16, transcendentals=0),
+        name="either",
+    )(far, late, passed)
     return pl.pallas_call(
         gradient,
         out_shape=jax.ShapeDtypeStruct((OWN_COLS, ROWS), f32),

time: 25.5 us -> 25.2 us (0.988)
  starting transfers between devices: 18 us -> 12.1 us
  waiting for transfers between devices: 1.42 us -> 7.09 us
    ppermute x1 -> x3, starting transfers between devices: 12.3 us -> 6.36 us  [the longest x1 4.42 us: on_device(): far = lax.ppermute(jnp.where(ends, late, to_far), axes, moves)]
    ppermute x1 -> x3, waiting for transfers between devices: 1.42 us -> 7.09 us  [the longest x1 5.66 us: on_device(): late = lax.ppermute(to_far, axes, [(t - 1, t) for t in starts])]
  transfers between devices with their start and end apart: 2 -> 4, of which waited for: 1 -> 2; matrix products, arithmetic and copies ran while one was open for 0% -> 0% of each run, Pallas kernels for 0% -> 0%
where the time goes in v5:
time: 25.2 us; the launch traced here: 24.9 us
  starting transfers between devices  12.1 us (48%)
  waiting for transfers between devices  7.09 us (28%)
  Pallas kernels  5.56 us (22%)
    all_to_all x1, starting transfers between devices, on_device(): messages = lax.all_to_all(message, ('core', 'kern'), 0, 0)  5.79 us
    ppermute x1, waiting for transfers between devices, on_device(): late = lax.ppermute(to_far, axes, [(t - 1, t) for t in starts])  5.66 us
    ppermute x1, starting transfers between devices, on_device(): far = lax.ppermute(jnp.where(ends, late, to_far), axes, moves)  4.42 us
    pallas_call x1, Pallas kernels, on_device(): pl.pallas_call(gradient, out_shape=jax.ShapeDtypeStruct((OWN_COLS, ROWS),...  3.72 us
    pallas_call x1, Pallas kernels, on_device(): pl.pallas_call(prepare, out_shape=(jax.ShapeDtypeStruct((ROWS, 128), f32)...  1.81 us
    ppermute x1, waiting for transfers between devices, on_device(): far = lax.ppermute(jnp.where(ends, late, to_far), axes, moves)  1.43 us
    ppermute x1, starting transfers between devices, on_device(): late = lax.ppermute(to_far, axes, [(t - 1, t) for t in starts])  1.29 us
    ppermute x1, starting transfers between devices, on_device(): passed = lax.ppermute(far, axes, [(t + RUN - 1, t - 1) for t in RELAYED])  0.65 us
  transfers between devices with their start and end apart: 4, of which 2 were waited for; matrix products, arithmetic and copies ran while one was open for 0% of the time, Pallas kernels for 0%

profile of v5, /device:TPU:56, one launch (start us, length us, event | category | flops | bytes accessed | tf_op | source)
XLA Modules:
  0.0 24.9 jit_solution(4582276884715014205)
XLA Ops:
  0.0 1.8 %prepare.1 = (f32[64,128]{1,0:T(8,128)S(1)}, f32[64,128]{1,0:T(8,128)S(1)}, bf16[64,128]{1,0:T(8,128)(2,1)S(1)}, bf16[16,8,1024]{2,1,0:T(8,128)(2,1)}) custom-call(s32[64,256]{1,0:T(8,128)} %levels_hbm.1, f32[64,256]{1,0:T(8,128)} %jitter_hbm.1, s32[64,256]{1,0:T(8,128)} %target_hbm.1, bf16[3,35,2,35]{3,2,1,0:T(2,128)(2,1)} %bitcast.2, f32[3]{0:T(128)} %weight_hbm.1), custom_call_target="tpu_custom_call" | custom-call | tf_op jit(solution)/shard_map/prepare/pallas_call | solution.py:231
  1.8 1.3 %collective-permute-start = (bf16[64,128]{1,0:T(8,128)(2,1)S(1)}, bf16[64,128]{1,0:T(8,128)(2,1)S(1)}, u32[]{:S(2)}, u32[]{:S(2)}) collective-permute-start(bf16[64,128]{1,0:T(8,128)(2,1)S(1)} %get-tuple-element.11), channel_id=1, source_target_pairs={{120,128},{248,256},{376,384},{121,129},{249,257},{377,385},{122,1... | collective-permute-start | bytes 49160 | tf_op jit(solution)/shard_map/ppermute | solution.py:259
  3.1 5.8 %all-to-all-start = ((bf16[16,8,1024]{2,1,0:T(8,128)(2,1)}), bf16[16,8,1024]{2,1,0:T(8,128)(2,1)S(1)}, u32[]{:S(2)}, u32[]{:S(2)}) async-start(bf16[16,8,1024]{2,1,0:T(8,128)(2,1)} %get-tuple-element.12), calls=%async_computation | async-start | bytes 524288 | tf_op jit(solution)/shard_map/all_to_all | solution.py:260
  8.9 5.7 %collective-permute-done.late_ref = bf16[64,128]{1,0:T(8,128)(2,1)S(1)} collective-permute-done((bf16[64,128]{1,0:T(8,128)(2,1)S(1)}, bf16[64,128]{1,0:T(8,128)(2,1)S(1)}, u32[]{:S(2)}, u32[]{:S(2)}) %collective-permute-start) | collective-permute-done | bytes 16416 | tf_op jit(solution)/shard_map/ppermute | solution.py:259
  14.6 4.4 %collective-permute-start.1 = (bf16[64,128]{1,0:T(8,128)(2,1)S(1)}, bf16[64,128]{1,0:T(8,128)(2,1)S(1)}, u32[]{:S(2)}, u32[]{:S(2)}) collective-permute-start(bf16[64,128]{1,0:T(8,128)(2,1)S(1)} %broadcast_select_fusion), channel_id=1, source_target_pairs={{8,16},{24,32},{40,48},{56,64},{72,80},{88,96},{104,112},{136,144}... | collective-permute-start | bytes 49160 | tf_op jit(solution)/shard_map/ppermute | solution.py:265
  19.0 1.4 %collective-permute-done.1.far_ref = bf16[64,128]{1,0:T(8,128)(2,1)S(1)} collective-permute-done((bf16[64,128]{1,0:T(8,128)(2,1)S(1)}, bf16[64,128]{1,0:T(8,128)(2,1)S(1)}, u32[]{:S(2)}, u32[]{:S(2)}) %collective-permute-start.1) | collective-permute-done | bytes 16416 | tf_op jit(solution)/shard_map/ppermute | solution.py:265
  20.4 0.7 %collective-permute-start.2 = (bf16[64,128]{1,0:T(8,128)(2,1)S(1)}, bf16[64,128]{1,0:T(8,128)(2,1)S(1)}, u32[]{:S(2)}, u32[]{:S(2)}) collective-permute-start(bf16[64,128]{1,0:T(8,128)(2,1)S(1)} %collective-permute-done.1.far_ref), channel_id=1, source_target_pairs={{376,248},{504,376},{377,249},{505,377},{378,250},{506,378},{379,2... | collective-permute-start | bytes 49160 | tf_op jit(solution)/shard_map/ppermute | solution.py:266
  21.1 0.0 collective-permute-done.2.passed_ref
  21.1 0.0 all-to-all-done.message_ref
  21.1 3.7 %gradient.1 = f32[32,64]{1,0:T(8,128)} custom-call(f32[64,128]{1,0:T(8,128)S(1)} %get-tuple-element.9.mask_ref, f32[64,128]{1,0:T(8,128)S(1)} %get-tuple-element.10.goal_ref, f32[64,128]{1,0:T(8,128)S(1)} %either.1.far_ref, bf16[16,8,1024]{2,1,0:T(8,128)(2,1)S(1)} %all-to-all-done.message_ref), custom_call_target="tpu_custom_call" | custom-call | tf_op jit(solution)/shard_map/gradient/pallas_call | solution.py:276
  (2 shorter events, 0.0 us)
Async XLA Ops:
  1.8 12.7 %collective-permute-start = (bf16[64,128]{1,0:T(8,128)(2,1)S(1)}, bf16[64,128]{1,0:T(8,128)(2,1)S(1)}, u32[]{:S(2)}, u32[]{:S(2)}) collective-permute-start(bf16[64,128]{1,0:T(8,128)(2,1)S(1)} %get-tuple-element.11), channel_id=1, source_target_pairs={{120,128},{248,256},{376,384},{121,129},{249,257},{377,385},{122,1... | collective-permute-start | bytes 49160 | tf_op jit(solution)/shard_map/ppermute | solution.py:259
  3.1 18.0 %all-to-all-start = ((bf16[16,8,1024]{2,1,0:T(8,128)(2,1)}), bf16[16,8,1024]{2,1,0:T(8,128)(2,1)S(1)}, u32[]{:S(2)}, u32[]{:S(2)}) async-start(bf16[16,8,1024]{2,1,0:T(8,128)(2,1)} %get-tuple-element.12), calls=%async_computation | async-start | bytes 524288 | tf_op jit(solution)/shard_map/all_to_all | solution.py:260
  14.6 5.9 %collective-permute-start.1 = (bf16[64,128]{1,0:T(8,128)(2,1)S(1)}, bf16[64,128]{1,0:T(8,128)(2,1)S(1)}, u32[]{:S(2)}, u32[]{:S(2)}) collective-permute-start(bf16[64,128]{1,0:T(8,128)(2,1)S(1)} %broadcast_select_fusion), channel_id=1, source_target_pairs={{8,16},{24,32},{40,48},{56,64},{72,80},{88,96},{104,112},{136,144}... | collective-permute-start | bytes 49160 | tf_op jit(solution)/shard_map/ppermute | solution.py:265
  20.4 0.7 %collective-permute-start.2 = (bf16[64,128]{1,0:T(8,128)(2,1)S(1)}, bf16[64,128]{1,0:T(8,128)(2,1)S(1)}, u32[]{:S(2)}, u32[]{:S(2)}) collective-permute-start(bf16[64,128]{1,0:T(8,128)(2,1)S(1)} %collective-permute-done.1.far_ref), channel_id=1, source_target_pairs={{376,248},{504,376},{377,249},{505,377},{378,250},{506,378},{379,2... | collective-permute-start | bytes 49160 | tf_op jit(solution)/shard_map/ppermute | solution.py:266

commit v6 on v5

--- a/solution.py
+++ b/solution.py
@@ -26,6 +26,7 @@
 ROWS = 64
 RUN = 16
 RELAYED = (32, 48)
+RELAY = 11
 LATE_COST = 33 * 10**8
 SHARE = 8
 HALF_FLAT = FLAT // 2
@@ -108,10 +109,7 @@
 
 
 def either(far_ref, late_ref, passed_ref, rows_ref):
-    tile = lax.axis_index("pair") * 2 + lax.axis_index("core")
     far = far_ref[...].astype(jnp.float32)
-    for start in RELAYED:
-        far = jnp.where(tile == start + RUN - 1, 0.0, far)
     rows_ref[...] = far + late_ref[...].astype(jnp.float32) + passed_ref[...].astype(jnp.float32)
 
 
@@ -260,10 +258,11 @@
     messages = lax.all_to_all(message, ("core", "kern"), 0, 0)
     meet = [(t, t + 1) for t in range(1, tiles - 1, 2)]
     moves = [(a, b) for a, b in meet if b not in starts]
-    moves += [(b, a) for a, b in meet if b not in RELAYED] + [(t, t + RUN - 1) for t in RELAYED]
+    moves += [(b, a) for a, b in meet if b not in RELAYED]
     ends = lax.axis_index(axes) % RUN == RUN - 1
-    far = lax.ppermute(jnp.where(ends, late, to_far), axes, moves)
-    passed = lax.ppermute(far, axes, [(t + RUN - 1, t - 1) for t in RELAYED])
+    relayed = lax.ppermute(jnp.where(ends, late, to_far), axes, [(t, t + RELAY) for t in RELAYED])
+    far = lax.ppermute(to_far, axes, moves)
+    passed = lax.ppermute(relayed, axes, [(t + RELAY, t - 1) for t in RELAYED])
     far = pl.pallas_call(
         either,
         out_shape=jax.ShapeDtypeStruct((ROWS, 128), f32),

time: 25.2 us -> 25.8 us (1.024)
  the two profiles are of different devices: /device:TPU:56 before, /device:TPU:467 now
where the time goes in v6:
time: 25.8 us; the launch traced here: 25.5 us
  waiting for transfers between devices  10.3 us (40%)
  starting transfers between devices  9.53 us (37%)
  Pallas kernels  5.54 us (21%)
    ppermute x1, waiting for transfers between devices, on_device(): passed = lax.ppermute(relayed, axes, [(t + RELAY, t - 1) for t in RELAYED])  10.3 us
    all_to_all x1, starting transfers between devices, on_device(): messages = lax.all_to_all(message, ('core', 'kern'), 0, 0)  5.63 us
    pallas_call x1, Pallas kernels, on_device(): pl.pallas_call(gradient, out_shape=jax.ShapeDtypeStruct((OWN_COLS, ROWS),...  3.72 us
    pallas_call x1, Pallas kernels, on_device(): pl.pallas_call(prepare, out_shape=(jax.ShapeDtypeStruct((ROWS, 128), f32)...  1.81 us
    ppermute x1, starting transfers between devices, on_device(): passed = lax.ppermute(relayed, axes, [(t + RELAY, t - 1) for t in RELAYED])  1.29 us
    ppermute x1, starting transfers between devices, on_device(): late = lax.ppermute(to_far, axes, [(t - 1, t) for t in starts])  1.29 us
    ppermute x1, starting transfers between devices, on_device(): lax.ppermute(jnp.where(ends, late, to_far), axes, [(t, t + RELAY) for t i...  0.66 us
    ppermute x1, starting transfers between devices, on_device(): far = lax.ppermute(to_far, axes, moves)  0.66 us
  transfers between devices with their start and end apart: 5, of which 1 were waited for; matrix products, arithmetic and copies ran while one was open for 0% of the time, Pallas kernels for 0%

profile of v6, /device:TPU:467, one launch (start us, length us, event | category | flops | bytes accessed | tf_op | source)
XLA Modules:
  0.0 25.5 jit_solution(15974137134789926897)
XLA Ops:
  0.0 1.8 %prepare.1 = (f32[64,128]{1,0:T(8,128)S(1)}, f32[64,128]{1,0:T(8,128)S(1)}, bf16[64,128]{1,0:T(8,128)(2,1)S(1)}, bf16[16,8,1024]{2,1,0:T(8,128)(2,1)}) custom-call(s32[64,256]{1,0:T(8,128)} %levels_hbm.1, f32[64,256]{1,0:T(8,128)} %jitter_hbm.1, s32[64,256]{1,0:T(8,128)} %target_hbm.1, bf16[3,35,2,35]{3,2,1,0:T(2,128)(2,1)} %bitcast.2, f32[3]{0:T(128)} %weight_hbm.1), custom_call_target="tpu_custom_call" | custom-call | tf_op jit(solution)/shard_map/prepare/pallas_call | solution.py:229
  1.8 1.3 %collective-permute-start.1 = (bf16[64,128]{1,0:T(8,128)(2,1)S(1)}, bf16[64,128]{1,0:T(8,128)(2,1)S(1)}, u32[]{:S(2)}, u32[]{:S(2)}) collective-permute-start(bf16[64,128]{1,0:T(8,128)(2,1)S(1)} %get-tuple-element.11), channel_id=1, source_target_pairs={{120,128},{248,256},{376,384},{121,129},{249,257},{377,385},{122,1... | collective-permute-start | bytes 49160 | tf_op jit(solution)/shard_map/ppermute | solution.py:257
  3.1 5.6 %all-to-all-start = ((bf16[16,8,1024]{2,1,0:T(8,128)(2,1)}), bf16[16,8,1024]{2,1,0:T(8,128)(2,1)S(1)}, u32[]{:S(2)}, u32[]{:S(2)}) async-start(bf16[16,8,1024]{2,1,0:T(8,128)(2,1)} %get-tuple-element.12), calls=%async_computation | async-start | bytes 524288 | tf_op jit(solution)/shard_map/all_to_all | solution.py:258
  8.7 0.0 collective-permute-done.1.late_ref
  8.8 0.7 %collective-permute-start.2 = (bf16[64,128]{1,0:T(8,128)(2,1)S(1)}, bf16[64,128]{1,0:T(8,128)(2,1)S(1)}, u32[]{:S(2)}, u32[]{:S(2)}) collective-permute-start(bf16[64,128]{1,0:T(8,128)(2,1)S(1)} %broadcast_select_fusion), channel_id=1, source_target_pairs={{256,344},{384,472},{257,345},{385,473},{258,346},{386,474},{259,3... | collective-permute-start | bytes 49160 | tf_op jit(solution)/shard_map/ppermute | solution.py:263
  9.4 0.7 %collective-permute-start = (bf16[64,128]{1,0:T(8,128)(2,1)S(1)}, bf16[64,128]{1,0:T(8,128)(2,1)S(1)}, u32[]{:S(2)}, u32[]{:S(2)}) collective-permute-start(bf16[64,128]{1,0:T(8,128)(2,1)S(1)} %get-tuple-element.11), channel_id=1, source_target_pairs={{8,16},{24,32},{40,48},{56,64},{72,80},{88,96},{104,112},{136,144}... | collective-permute-start | bytes 49160 | tf_op jit(solution)/shard_map/ppermute | solution.py:264
  10.1 0.0 collective-permute-done.2
  10.1 1.3 %collective-permute-start.3 = (bf16[64,128]{1,0:T(8,128)(2,1)S(1)}, bf16[64,128]{1,0:T(8,128)(2,1)S(1)}, u32[]{:S(2)}, u32[]{:S(2)}) collective-permute-start(bf16[64,128]{1,0:T(8,128)(2,1)S(1)} %collective-permute-done.2), channel_id=1, source_target_pairs={{344,248},{472,376},{345,249},{473,377},{346,250},{474,378},{347,2... | collective-permute-start | bytes 49160 | tf_op jit(solution)/shard_map/ppermute | solution.py:265
  11.4 0.0 collective-permute-done.far_ref
  11.4 10.3 %collective-permute-done.3.passed_ref = bf16[64,128]{1,0:T(8,128)(2,1)S(1)} collective-permute-done((bf16[64,128]{1,0:T(8,128)(2,1)S(1)}, bf16[64,128]{1,0:T(8,128)(2,1)S(1)}, u32[]{:S(2)}, u32[]{:S(2)}) %collective-permute-start.3) | collective-permute-done | bytes 16416 | tf_op jit(solution)/shard_map/ppermute | solution.py:265
  21.8 0.0 all-to-all-done.message_ref
  21.8 3.7 %gradient.1 = f32[32,64]{1,0:T(8,128)} custom-call(f32[64,128]{1,0:T(8,128)S(1)} %get-tuple-element.9.mask_ref, f32[64,128]{1,0:T(8,128)S(1)} %get-tuple-element.10.goal_ref, f32[64,128]{1,0:T(8,128)S(1)} %either.1.far_ref, bf16[16,8,1024]{2,1,0:T(8,128)(2,1)S(1)} %all-to-all-done.message_ref), custom_call_target="tpu_custom_call" | custom-call | tf_op jit(solution)/shard_map/gradient/pallas_call | solution.py:275
  (2 shorter events, 0.0 us)
Async XLA Ops:
  1.8 6.9 %collective-permute-start.1 = (bf16[64,128]{1,0:T(8,128)(2,1)S(1)}, bf16[64,128]{1,0:T(8,128)(2,1)S(1)}, u32[]{:S(2)}, u32[]{:S(2)}) collective-permute-start(bf16[64,128]{1,0:T(8,128)(2,1)S(1)} %get-tuple-element.11), channel_id=1, source_target_pairs={{120,128},{248,256},{376,384},{121,129},{249,257},{377,385},{122,1... | collective-permute-start | bytes 49160 | tf_op jit(solution)/shard_map/ppermute | solution.py:257
  3.1 18.7 %all-to-all-start = ((bf16[16,8,1024]{2,1,0:T(8,128)(2,1)}), bf16[16,8,1024]{2,1,0:T(8,128)(2,1)S(1)}, u32[]{:S(2)}, u32[]{:S(2)}) async-start(bf16[16,8,1024]{2,1,0:T(8,128)(2,1)} %get-tuple-element.12), calls=%async_computation | async-start | bytes 524288 | tf_op jit(solution)/shard_map/all_to_all | solution.py:258
  8.8 1.3 %collective-permute-start.2 = (bf16[64,128]{1,0:T(8,128)(2,1)S(1)}, bf16[64,128]{1,0:T(8,128)(2,1)S(1)}, u32[]{:S(2)}, u32[]{:S(2)}) collective-permute-start(bf16[64,128]{1,0:T(8,128)(2,1)S(1)} %broadcast_select_fusion), channel_id=1, source_target_pairs={{256,344},{384,472},{257,345},{385,473},{258,346},{386,474},{259,3... | collective-permute-start | bytes 49160 | tf_op jit(solution)/shard_map/ppermute | solution.py:263
  9.4 2.0 %collective-permute-start = (bf16[64,128]{1,0:T(8,128)(2,1)S(1)}, bf16[64,128]{1,0:T(8,128)(2,1)S(1)}, u32[]{:S(2)}, u32[]{:S(2)}) collective-permute-start(bf16[64,128]{1,0:T(8,128)(2,1)S(1)} %get-tuple-element.11), channel_id=1, source_target_pairs={{8,16},{24,32},{40,48},{56,64},{72,80},{88,96},{104,112},{136,144}... | collective-permute-start | bytes 49160 | tf_op jit(solution)/shard_map/ppermute | solution.py:264
  10.1 11.6 %collective-permute-start.3 = (bf16[64,128]{1,0:T(8,128)(2,1)S(1)}, bf16[64,128]{1,0:T(8,128)(2,1)S(1)}, u32[]{:S(2)}, u32[]{:S(2)}) collective-permute-start(bf16[64,128]{1,0:T(8,128)(2,1)S(1)} %collective-permute-done.2), channel_id=1, source_target_pairs={{344,248},{472,376},{345,249},{473,377},{346,250},{474,378},{347,2... | collective-permute-start | bytes 49160 | tf_op jit(solution)/shard_map/ppermute | solution.py:265

commit v7 on v5

--- a/solution.py
+++ b/solution.py
@@ -177,7 +177,7 @@
     row_in_clip = at + tile * ROWS
     row_ok = (row_in_clip >= 0) & (row_in_clip < tiles * ROWS)
     step = lax.broadcasted_iota(jnp.int32, (GROUP, 128), 0)
-    for first in range(0, FIELD_BLOCKS, 2):
+    for first in (FIELD_BLOCKS - 1, *range(0, FIELD_BLOCKS - 1, 2)):
         count = min(2, FIELD_BLOCKS - first)
         groups = min(GROUP, FIELD_COLS - GROUP * first)
         together = jnp.dot(

time: 25.2 us -> 25.1 us (level)
  no operation moved by 1% of the time
where the time goes in v7:
time: 25.1 us; the launch traced here: 24.8 us
  starting transfers between devices  12.1 us (48%)
  waiting for transfers between devices  7.09 us (28%)
  Pallas kernels  5.5 us (22%)
    all_to_all x1, starting transfers between devices, on_device(): messages = lax.all_to_all(message, ('core', 'kern'), 0, 0)  5.79 us
    ppermute x1, waiting for transfers between devices, on_device(): late = lax.ppermute(to_far, axes, [(t - 1, t) for t in starts])  5.66 us
    ppermute x1, starting transfers between devices, on_device(): far = lax.ppermute(jnp.where(ends, late, to_far), axes, moves)  4.42 us
    pallas_call x1, Pallas kernels, on_device(): pl.pallas_call(gradient, out_shape=jax.ShapeDtypeStruct((OWN_COLS, ROWS),...  3.67 us
    pallas_call x1, Pallas kernels, on_device(): pl.pallas_call(prepare, out_shape=(jax.ShapeDtypeStruct((ROWS, 128), f32)...  1.81 us
    ppermute x1, waiting for transfers between devices, on_device(): far = lax.ppermute(jnp.where(ends, late, to_far), axes, moves)  1.43 us
    ppermute x1, starting transfers between devices, on_device(): late = lax.ppermute(to_far, axes, [(t - 1, t) for t in starts])  1.29 us
    ppermute x1, starting transfers between devices, on_device(): passed = lax.ppermute(far, axes, [(t + RUN - 1, t - 1) for t in RELAYED])  0.65 us
  transfers between devices with their start and end apart: 4, of which 2 were waited for; matrix products, arithmetic and copies ran while one was open for 0% of the time, Pallas kernels for 0%

profile of v7, /device:TPU:56, one launch (start us, length us, event | category | flops | bytes accessed | tf_op | source)
XLA Modules:
  0.0 24.8 jit_solution(16467144350376368260)
XLA Ops:
  0.0 1.8 %prepare.1 = (f32[64,128]{1,0:T(8,128)S(1)}, f32[64,128]{1,0:T(8,128)S(1)}, bf16[64,128]{1,0:T(8,128)(2,1)S(1)}, bf16[16,8,1024]{2,1,0:T(8,128)(2,1)}) custom-call(s32[64,256]{1,0:T(8,128)} %levels_hbm.1, f32[64,256]{1,0:T(8,128)} %jitter_hbm.1, s32[64,256]{1,0:T(8,128)} %target_hbm.1, bf16[3,35,2,35]{3,2,1,0:T(2,128)(2,1)} %bitcast.2, f32[3]{0:T(128)} %weight_hbm.1), custom_call_target="tpu_custom_call" | custom-call | tf_op jit(solution)/shard_map/prepare/pallas_call | solution.py:231
  1.8 1.3 %collective-permute-start = (bf16[64,128]{1,0:T(8,128)(2,1)S(1)}, bf16[64,128]{1,0:T(8,128)(2,1)S(1)}, u32[]{:S(2)}, u32[]{:S(2)}) collective-permute-start(bf16[64,128]{1,0:T(8,128)(2,1)S(1)} %get-tuple-element.11), channel_id=1, source_target_pairs={{120,128},{248,256},{376,384},{121,129},{249,257},{377,385},{122,1... | collective-permute-start | bytes 49160 | tf_op jit(solution)/shard_map/ppermute | solution.py:259
  3.1 5.8 %all-to-all-start = ((bf16[16,8,1024]{2,1,0:T(8,128)(2,1)}), bf16[16,8,1024]{2,1,0:T(8,128)(2,1)S(1)}, u32[]{:S(2)}, u32[]{:S(2)}) async-start(bf16[16,8,1024]{2,1,0:T(8,128)(2,1)} %get-tuple-element.12), calls=%async_computation | async-start | bytes 524288 | tf_op jit(solution)/shard_map/all_to_all | solution.py:260
  8.9 5.7 %collective-permute-done.late_ref = bf16[64,128]{1,0:T(8,128)(2,1)S(1)} collective-permute-done((bf16[64,128]{1,0:T(8,128)(2,1)S(1)}, bf16[64,128]{1,0:T(8,128)(2,1)S(1)}, u32[]{:S(2)}, u32[]{:S(2)}) %collective-permute-start) | collective-permute-done | bytes 16416 | tf_op jit(solution)/shard_map/ppermute | solution.py:259
  14.6 4.4 %collective-permute-start.1 = (bf16[64,128]{1,0:T(8,128)(2,1)S(1)}, bf16[64,128]{1,0:T(8,128)(2,1)S(1)}, u32[]{:S(2)}, u32[]{:S(2)}) collective-permute-start(bf16[64,128]{1,0:T(8,128)(2,1)S(1)} %broadcast_select_fusion), channel_id=1, source_target_pairs={{8,16},{24,32},{40,48},{56,64},{72,80},{88,96},{104,112},{136,144}... | collective-permute-start | bytes 49160 | tf_op jit(solution)/shard_map/ppermute | solution.py:265
  19.0 1.4 %collective-permute-done.1.far_ref = bf16[64,128]{1,0:T(8,128)(2,1)S(1)} collective-permute-done((bf16[64,128]{1,0:T(8,128)(2,1)S(1)}, bf16[64,128]{1,0:T(8,128)(2,1)S(1)}, u32[]{:S(2)}, u32[]{:S(2)}) %collective-permute-start.1) | collective-permute-done | bytes 16416 | tf_op jit(solution)/shard_map/ppermute | solution.py:265
  20.4 0.7 %collective-permute-start.2 = (bf16[64,128]{1,0:T(8,128)(2,1)S(1)}, bf16[64,128]{1,0:T(8,128)(2,1)S(1)}, u32[]{:S(2)}, u32[]{:S(2)}) collective-permute-start(bf16[64,128]{1,0:T(8,128)(2,1)S(1)} %collective-permute-done.1.far_ref), channel_id=1, source_target_pairs={{376,248},{504,376},{377,249},{505,377},{378,250},{506,378},{379,2... | collective-permute-start | bytes 49160 | tf_op jit(solution)/shard_map/ppermute | solution.py:266
  21.1 0.0 collective-permute-done.2.passed_ref
  21.1 0.0 all-to-all-done.message_ref
  21.1 3.7 %gradient.1 = f32[32,64]{1,0:T(8,128)} custom-call(f32[64,128]{1,0:T(8,128)S(1)} %get-tuple-element.9.mask_ref, f32[64,128]{1,0:T(8,128)S(1)} %get-tuple-element.10.goal_ref, f32[64,128]{1,0:T(8,128)S(1)} %either.1.far_ref, bf16[16,8,1024]{2,1,0:T(8,128)(2,1)S(1)} %all-to-all-done.message_ref), custom_call_target="tpu_custom_call" | custom-call | tf_op jit(solution)/shard_map/gradient/pallas_call | solution.py:276
  (2 shorter events, 0.0 us)
Async XLA Ops:
  1.8 12.7 %collective-permute-start = (bf16[64,128]{1,0:T(8,128)(2,1)S(1)}, bf16[64,128]{1,0:T(8,128)(2,1)S(1)}, u32[]{:S(2)}, u32[]{:S(2)}) collective-permute-start(bf16[64,128]{1,0:T(8,128)(2,1)S(1)} %get-tuple-element.11), channel_id=1, source_target_pairs={{120,128},{248,256},{376,384},{121,129},{249,257},{377,385},{122,1... | collective-permute-start | bytes 49160 | tf_op jit(solution)/shard_map/ppermute | solution.py:259
  3.1 18.0 %all-to-all-start = ((bf16[16,8,1024]{2,1,0:T(8,128)(2,1)}), bf16[16,8,1024]{2,1,0:T(8,128)(2,1)S(1)}, u32[]{:S(2)}, u32[]{:S(2)}) async-start(bf16[16,8,1024]{2,1,0:T(8,128)(2,1)} %get-tuple-element.12), calls=%async_computation | async-start | bytes 524288 | tf_op jit(solution)/shard_map/all_to_all | solution.py:260
  14.6 5.9 %collective-permute-start.1 = (bf16[64,128]{1,0:T(8,128)(2,1)S(1)}, bf16[64,128]{1,0:T(8,128)(2,1)S(1)}, u32[]{:S(2)}, u32[]{:S(2)}) collective-permute-start(bf16[64,128]{1,0:T(8,128)(2,1)S(1)} %broadcast_select_fusion), channel_id=1, source_target_pairs={{8,16},{24,32},{40,48},{56,64},{72,80},{88,96},{104,112},{136,144}... | collective-permute-start | bytes 49160 | tf_op jit(solution)/shard_map/ppermute | solution.py:265
  20.4 0.7 %collective-permute-start.2 = (bf16[64,128]{1,0:T(8,128)(2,1)S(1)}, bf16[64,128]{1,0:T(8,128)(2,1)S(1)}, u32[]{:S(2)}, u32[]{:S(2)}) collective-permute-start(bf16[64,128]{1,0:T(8,128)(2,1)S(1)} %collective-permute-done.1.far_ref), channel_id=1, source_target_pairs={{376,248},{504,376},{377,249},{505,377},{378,250},{506,378},{379,2... | collective-permute-start | bytes 49160 | tf_op jit(solution)/shard_map/ppermute | solution.py:266
